TPU v7x, 512 devices: a whole 4x8x8 slice. The times are simulated.
512 devices in a mesh: rows: 128 (over z, y_hi, x, core), heads: 4 (over y_lo).
Axes of the slice: x: 4, y: 8 (y_hi: 2, y_lo: 4; y = y_hi * 4 + y_lo), z: 8, core: 2. Of those that a mesh axis runs over, the one named last changes fastest.
Arguments:
- features: bfloat16 [1024, 128, 384], P('heads', 'rows'), may hold values from -6 to 6
- cotangent: bfloat16 [1024, 128, 384], P('heads', 'rows'), may hold values from -0.59765625 to 0.59765625
- inject_row: bfloat16 [64, 128, 384], P(None, 'rows'), may hold values from -0.75 to 0.75
- readout_row: bfloat16 [64, 128, 384], P(None, 'rows'), may hold values from -3 to 3
- inject_col: bfloat16 [64, 128, 384], P(None, 'rows'), may hold values from -0.75 to 0.75
- readout_col: bfloat16 [64, 128, 384], P(None, 'rows'), may hold values from -3 to 3
- decay_row: bfloat16 [16, 128, 384], P('heads', 'rows'), may hold values from -0.8 to 0
- decay_col: bfloat16 [16, 128, 384], P('heads', 'rows'), may hold values from -0.8 to 0
- tissue: int32 [128, 24], P('rows'), may hold values 0 or 1
Outputs:
- grad_features: bfloat16 [1024, 128, 384], P('heads', 'rows')
- grad_inject_row: bfloat16 [64, 128, 384], P('heads', 'rows')
- grad_readout_row: bfloat16 [64, 128, 384], P('heads', 'rows')
- grad_inject_col: bfloat16 [64, 128, 384], P('heads', 'rows')
- grad_readout_col: bfloat16 [64, 128, 384], P('heads', 'rows')
- grad_decay_row: bfloat16 [16, 128, 384], P('heads', 'rows')
- grad_decay_col: bfloat16 [16, 128, 384], P('heads', 'rows')
All inputs are finite; a program needn't handle non-finite values. No bound on the sum of `tissue` on one device may be relied on, other than what follows from the above.
Results may differ from a plain program's by a relative error of at most 0.005.
Values may be sent and summed in bfloat16 or wider, within the bound.
No kernel may reach another device: no remote copies, remote signals or barrier semaphores. Data moves between devices by JAX's collectives and lax.ppermute only.
A program may use at most 64 MiB of HBM per device.

v0:
```python
from functools import partial

import jax
import jax.numpy as jnp
from jax import lax
from jax.experimental import pallas as pl
from jax.experimental.pallas import tpu as pltpu
from jax.sharding import PartitionSpec as P

TILE = 16
L = 128
HD = 64
F32, BF16 = jnp.float32, jnp.bfloat16


def nn(a, b):
    return lax.dot_general(a, b, (((1,), (0,)), ((), ())), preferred_element_type=F32)


def nt(a, b):
    return lax.dot_general(a, b, (((1,), (1,)), ((), ())), preferred_element_type=F32)


def tn(a, b):
    return lax.dot_general(a, b, (((0,), (0,)), ((), ())), preferred_element_type=F32)


def upper(dtype):
    i = lax.broadcasted_iota(jnp.int32, (L, L), 0)
    j = lax.broadcasted_iota(jnp.int32, (L, L), 1)
    return (i <= j).astype(dtype)


def split3(x):
    hi = x.astype(BF16)
    r = x - hi.astype(F32)
    mid = r.astype(BF16)
    return hi, mid, (r - mid.astype(F32)).astype(BF16)


def keep_of(tissue, n):
    tiles = tissue.shape[1]
    t = lax.broadcasted_iota(jnp.int32, (tiles, n), 0) * TILE
    j = lax.broadcasted_iota(jnp.int32, (tiles, n), 1)
    spread = ((j >= t) & (j < t + TILE)).astype(F32)
    rows = jnp.broadcast_to(tissue.astype(F32), (8, tiles))
    return nn(rows, spread)[0:1]


def prep_kernel(x_ref, w_ref, u_ref, v_ref, a_ref, tis_ref, send_ref, xm_ref, wm_ref, wt_ref, scr):
    n = x_ref.shape[1]
    blocks = n // L
    keep = keep_of(tis_ref[...], n).astype(BF16)
    xm_ref[...] = x_ref[...] * keep
    wm_ref[...] = w_ref[...] * keep
    halves = x_ref.shape[0] // L
    per = 2 * halves + 1
    for k in range(blocks):
        at = pl.ds(k * L, L)
        for r in range(halves):
            ch = pl.ds(r * L, L)
            scr[:, per * k + r, :] = xm_ref[ch, at].astype(F32).T
            wt = wm_ref[ch, at].astype(F32).T
            scr[:, per * k + halves + r, :] = wt
            wt_ref[at, ch] = wt.astype(BF16)
        uv = jnp.concatenate([u_ref[:, at].astype(F32), v_ref[:, at].astype(F32)], axis=0)
        scr[:, per * k + 2 * halves, :] = uv.T
    heads = a_ref.shape[0]
    a = [a_ref[:, pl.ds(k * L, L)].astype(F32) for k in range(blocks)]
    a.append(jnp.zeros((L - heads * blocks, L), F32))
    scr[:, per * blocks, :] = jnp.concatenate(a, axis=0).T
    send_ref[...] = scr[...].astype(BF16)


def row_kernel(xm_ref, wm_ref, wt_ref, u_ref, v_ref, a_ref, dx_ref, d0_ref, d1_ref, d2_ref, d3_ref, da_ref, y_ref, duv_ref):
    n = xm_ref.shape[1]
    blocks = n // L
    heads = a_ref.shape[0]
    nstate = u_ref.shape[0]
    tri = upper(BF16)
    le = upper(F32)
    carry = jnp.zeros((heads, 1), F32)
    grow, gcol = [], []
    for b in range(blocks):
        g = nn(a_ref[:, pl.ds(b * L, L)], tri) + carry
        carry = g[:, L - 1 : L]
        grow.append(g)
        gcol.append(jnp.concatenate([g, jnp.zeros((8 - heads, L), F32)], axis=0).T)
    vt = [v_ref[:, pl.ds(b * L, L)].astype(F32).T.astype(BF16) for b in range(blocks)]
    i0 = lax.broadcasted_iota(jnp.int32, (L, L), 0)
    i1 = lax.broadcasted_iota(jnp.int32, (L, L), 1)
    lower = i1 <= i0
    dv = [None] * blocks
    du = [None] * blocks
    for j in range(blocks):
        sj = pl.ds(j * L, L)
        dxs = [None] * heads
        for i in range(j, blocks):
            ti = pl.ds(i * L, L)
            s = nn(vt[i], u_ref[:, sj])
            q = None
            for h in range(heads):
                ch = pl.ds(h * HD, HD)
                d = jnp.exp(jnp.minimum(gcol[i][:, h : h + 1] - grow[j][h : h + 1, :], 0.0))
                if i == j:
                    d = jnp.where(lower, d, 0.0)
                m = nn(wt_ref[ti, ch], xm_ref[ch, sj])
                dm = d * m
                q = dm if q is None else q + dm
                a = (d * s).astype(BF16)
                part = nn(wm_ref[ch, ti], a)
                dxs[h] = part if dxs[h] is None else dxs[h] + part
                y = nt(xm_ref[ch, sj], a)
                if j == 0:
                    y_ref[ch, ti] = y
                else:
                    y_ref[ch, ti] += y
            qb = q.astype(BF16)
            pu = nn(v_ref[:, ti], qb)
            pv = nt(u_ref[:, sj], qb)
            du[j] = pu if du[j] is None else du[j] + pu
            dv[i] = pv if dv[i] is None else dv[i] + pv
        for h in range(heads):
            dx_ref[pl.ds(h * HD, HD), sj] = dxs[h]
    quarter = nstate // 4
    for b in range(blocks):
        at = pl.ds(b * L, L)
        for k in range(4):
            duv_ref[pl.ds(2 * quarter * k, quarter), at] = du[b][quarter * k : quarter * (k + 1)]
            duv_ref[pl.ds(2 * quarter * k + quarter, quarter), at] = dv[b][quarter * k : quarter * (k + 1)]
    me = lax.axis_index("heads")
    for shift, ref in enumerate((d0_ref, d1_ref, d2_ref, d3_ref)):
        part = lax.rem(me + shift, 4) * (2 * quarter)
        ref[...] = duv_ref[pl.ds(pl.multiple_of(part, 2 * quarter), 2 * quarter), :].astype(ref.dtype)
    suffix = (i0 >= i1).astype(BF16)
    later = jnp.zeros((heads, 1), F32)
    for b in reversed(range(blocks)):
        at = pl.ds(b * L, L)
        e = wm_ref[:, at].astype(F32) * y_ref[:, at] - xm_ref[:, at].astype(F32) * dx_ref[:, at]
        dg = jnp.sum(e.reshape(heads, HD, L), axis=1)
        hi, mid, lo = split3(dg)
        da = nn(hi, suffix) + nn(mid, suffix) + nn(lo, suffix) + later
        later = da[:, 0:1]
        da_ref[:, at] = da.astype(BF16)


def col_pair_kernel(recv_ref, after_ref, hop_ref, a_ref, xt_ref, wt_ref, scr, *, blocks, heads):
    scr[...] = recv_ref[...].astype(F32)
    halves = heads // 2
    per = 2 * halves + 1
    tri = upper(BF16)
    i0 = lax.broadcasted_iota(jnp.int32, (L, L), 0)
    i1 = lax.broadcasted_iota(jnp.int32, (L, L), 1)
    later = i0 <= i1
    gcol = tn(tri, scr[:, per * blocks, :].astype(BF16))
    grow = gcol.T
    for k in range(blocks):
        for r in range(halves):
            xt_ref[k, :, pl.ds(r * L, L)] = scr[:, per * k + r, :].astype(BF16)
            wt_ref[k, :, pl.ds(r * L, L)] = scr[:, per * k + halves + r, :].astype(BF16)
        uvt = scr[:, per * k + 2 * halves, :]
        uv = uvt.T.astype(BF16)
        u, v = uv[:HD], uv[HD:]
        s = nn(uvt[:, :HD].astype(BF16), v)
        q = None
        for h in range(heads):
            ch = pl.ds(h * HD, HD)
            c = heads * k + h
            d = jnp.exp(jnp.minimum(grow[c : c + 1, :] - gcol[:, c : c + 1], 0.0))
            d = jnp.where(later, d, 0.0)
            m = nt(xt_ref[k, :, ch], wt_ref[k, :, ch])
            dm = d * m
            q = dm if q is None else q + dm
            a_ref[c] = (d * s).astype(BF16)
        qb = q.astype(BF16)
        du = nt(v, qb).astype(BF16)
        dv = nn(u, qb).astype(BF16)
        quarter = HD // 4
        for p in range(4):
            hop_ref[p, pl.ds(2 * quarter * k, quarter), :] = du[quarter * p : quarter * (p + 1)]
            hop_ref[p, pl.ds(2 * quarter * k + quarter, quarter), :] = dv[quarter * p : quarter * (p + 1)]


def col_value_kernel(a_ref, xt_ref, wt_ref, ret_ref, da_ref, y_ref, dx_ref, *, blocks, heads):
    i0 = lax.broadcasted_iota(jnp.int32, (L, L), 0)
    i1 = lax.broadcasted_iota(jnp.int32, (L, L), 1)
    suffix = (i0 >= i1).astype(BF16)
    rows = da_ref.shape[0]
    width = heads * HD
    c0 = lax.broadcasted_iota(jnp.int32, (rows, width), 0)
    c1 = lax.broadcasted_iota(jnp.int32, (rows, width), 1)
    dg = jnp.zeros((rows, L), F32)
    for k in range(blocks):
        for h in range(heads):
            ch = pl.ds(h * HD, HD)
            a = a_ref[heads * k + h]
            dx_ref[:, ch] = nn(a, wt_ref[k, :, ch])
            y_ref[:, ch] = tn(a, xt_ref[k, :, ch])
        dx = dx_ref[...]
        for r in range(heads // 2):
            ret_ref[:, (heads // 2) * k + r, :] = dx[:, r * L : (r + 1) * L]
        e = wt_ref[k].astype(F32) * y_ref[...] - xt_ref[k].astype(F32) * dx
        start = (c0 - heads * k) * HD
        seg = ((c1 >= start) & (c1 < start + HD)).astype(BF16)
        for part in split3(e):
            dg += nt(seg, part)
    hi, mid, lo = split3(dg)
    da_ref[...] = nn(hi, suffix) + nn(mid, suffix) + nn(lo, suffix)


def pack_kernel(hop_ref, ret_ref, da_ref, out_ref, scr, *, used):
    total = hop_ref[0].astype(F32)
    for p in range(1, 4):
        total += hop_ref[p].astype(F32)
    rows = total.shape[0] + da_ref.shape[0]
    small = [total, da_ref[...], jnp.zeros((L - rows, L), F32)]
    scr[...] = ret_ref[...]
    scr[:, used, :] = jnp.concatenate(small, axis=0).T
    scr[:, used + 1, :] = jnp.zeros((L, L), F32)
    out_ref[...] = scr[...].astype(BF16)


def final_kernel(back_ref, dx_ref, tis_ref, r0_ref, r1_ref, r2_ref, r3_ref, gx_ref, iu_ref, iv_ref, cu_ref, cv_ref, da_ref, scr, *, heads):
    n = dx_ref.shape[1]
    blocks = n // L
    halves = heads // 2
    keep = keep_of(tis_ref[...], n)
    scr[...] = back_ref[...].astype(F32)
    for k in range(blocks):
        at = pl.ds(k * L, L)
        for r in range(halves):
            ch = pl.ds(r * L, L)
            both = dx_ref[ch, at] + scr[:, halves * k + r, :].T
            gx_ref[ch, at] = (both * keep[:, k * L : (k + 1) * L]).astype(BF16)
    small = scr[:, halves * blocks, :].T
    quarter = cu_ref.shape[0]
    for k in range(blocks):
        at = pl.ds(k * L, L)
        o = 2 * quarter * k
        cu_ref[:, at] = small[o : o + quarter].astype(BF16)
        cv_ref[:, at] = small[o + quarter : o + 2 * quarter].astype(BF16)
        o = 2 * quarter * blocks + heads * k
        da_ref[:, at] = small[o : o + heads].astype(BF16)
    row = r0_ref[...] + r1_ref[...].astype(F32) + r2_ref[...].astype(F32) + r3_ref[...].astype(F32)
    iu_ref[...] = row[:quarter].astype(BF16)
    iv_ref[...] = row[quarter:].astype(BF16)


def call(kernel, outs, scratch, flops, moved, name, in_specs=None):
    more = {} if in_specs is None else {"in_specs": in_specs}
    return pl.pallas_call(
        kernel,
        **more,
        out_shape=[jax.ShapeDtypeStruct(s, d) for s, d in outs],
        scratch_shapes=[pltpu.VMEM(s, F32) for s in scratch],
        compiler_params=pltpu.CompilerParams(vmem_limit_bytes=32 * 2**20),
        cost_estimate=pl.CostEstimate(flops=flops, bytes_accessed=moved, transcendentals=0),
        name=name,
    )


def body(features, cotangent, inject_row, readout_row, inject_col, readout_col, decay_row, decay_col, tissue):
    heads = decay_row.shape[0]
    chan, _, n = features.shape
    nstate = inject_row.shape[0]
    blocks = n // L
    flat = lambda x: x.reshape(x.shape[0], n)
    x, w = flat(features), flat(cotangent)
    per = 2 * chan // L + 1
    rows_out = per * blocks + 1
    send, xm, wm, wt = call(
        prep_kernel,
        [((L, rows_out, L), BF16), ((chan, n), BF16), ((chan, n), BF16), ((n, chan), BF16)],
        [(L, rows_out, L)],
        10**7, 10**6, "pack_rows",
    )(x, w, flat(inject_col), flat(readout_col), flat(decay_col), tissue)
    recv = lax.all_to_all(send, "rows", split_axis=0, concat_axis=0, tiled=True)
    share = (nstate // 2, n)
    dx_row, mine, *theirs, da_row = call(
        row_kernel,
        [((chan, n), F32), (share, F32), (share, BF16), (share, BF16), (share, BF16), ((heads, n), BF16)],
        [(chan, n), (2 * nstate, n)],
        4 * 10**9, 10**6, "row_scan",
    )(xm, wm, wt, flat(inject_row), flat(readout_row), flat(decay_row))
    shares = [
        lax.ppermute(part, "heads", [(i, (i + shift) % 4) for i in range(4)]) for shift, part in enumerate(theirs, 1)
    ]
    sizes = dict(blocks=blocks, heads=heads)
    hop, weights, xt, wtc = call(
        partial(col_pair_kernel, **sizes),
        [((4, nstate // 2 * blocks, L), BF16), ((blocks * heads, L, L), BF16), ((blocks, L, chan), BF16), ((blocks, L, chan), BF16)],
        [(L, rows_out, L)],
        10**9, 10**6, "col_pairs",
        [pl.BlockSpec(memory_space=pltpu.VMEM), pl.BlockSpec(memory_space=pl.ANY)],
    )(recv, da_row)
    hopped = lax.all_to_all(hop, "heads", split_axis=0, concat_axis=0, tiled=True)
    used = blocks * heads // 2
    ret, da_col = call(
        partial(col_value_kernel, **sizes),
        [((L, used + 2, L), F32), ((16, L), F32)],
        [(L, chan), (L, chan)],
        2 * 10**9, 10**6, "col_values",
    )(weights, xt, wtc)
    (packed,) = call(
        partial(pack_kernel, used=used), [((L, used + 2, L), BF16)], [(L, used + 2, L)], 10**7, 10**6, "pack_cols"
    )(hopped, ret, da_col)
    back = lax.all_to_all(packed, "rows", split_axis=0, concat_axis=0, tiled=True)
    quarter = nstate // 4
    gx, iu, iv, cu, cv, da = call(
        partial(final_kernel, heads=heads),
        [((chan, n), BF16)] + [((quarter, n), BF16)] * 4 + [((heads, n), BF16)],
        [(L, used + 2, L)],
        10**7, 10**6, "join",
    )(back, dx_row, tissue, mine, *shares)
    wide = lambda x: x.reshape(x.shape[0], 1, n)
    return wide(gx), wide(iu), wide(iv), wide(cu), wide(cv), wide(da_row), wide(da)


def solution(mesh):
    split = P("heads", "rows", None)
    shared = P(None, "rows", None)
    in_specs = (split, split, shared, shared, shared, shared, split, split, P("rows", None))
    return jax.shard_map(body, mesh=mesh, in_specs=in_specs, out_specs=(split,) * 7, check_vma=False)
```

profile of v0, /device:TPU:9, one launch (start us, length us, event | category | flops | bytes accessed | tf_op | source)
XLA Modules:
  0.0 88.2 jit_solution(11430530077599104245)
XLA Ops:
  0.6 0.0 copy-start.4
  0.6 0.0 copy-start.5
  0.7 0.7 copy-done.4
  1.3 0.0 copy-done.5
  1.3 0.0 copy-start
  1.3 0.9 %copy-done = bf16[256,1,384]{2,0,1:T(8,128)(2,1)S(1)} copy-done((bf16[256,1,384]{2,0,1:T(8,128)(2,1)S(1)}, bf16[256,1,384]{2,0,1:T(8,128)(2,1)}, u32[]{:S(2)}) %copy-start) | copy-done | bytes 196632
  2.3 0.9 %copy-done.1 = bf16[256,1,384]{2,0,1:T(8,128)(2,1)S(1)} copy-done((bf16[256,1,384]{2,0,1:T(8,128)(2,1)S(1)}, bf16[256,1,384]{2,0,1:T(8,128)(2,1)}, u32[]{:S(2)}) %copy-start.1) | copy-done | bytes 196632
  3.2 0.8 copy-done.2
  4.0 0.8 copy-done.3
  4.8 1.7 %pack_rows.1 = (bf16[128,16,128]{2,1,0:T(8,128)(2,1)}, bf16[256,384]{1,0:T(8,128)(2,1)S(1)}, bf16[256,384]{1,0:T(8,128)(2,1)S(1)}, bf16[384,256]{1,0:T(8,128)(2,1)S(1)}) custom-call(bf16[256,384]{1,0:T(8,128)(2,1)S(1)} %bitcast.15, bf16[256,384]{1,0:T(8,128)(2,1)S(1)} %bitcast.16, bf16[64,384]{1,0:T(8,128)(2,1)S(1)} %bitcast.17, ...), custom_call_target="tpu_custom_call" | custom-call | flops 10000000 | bytes 1000000 | tf_op jit(solution)/shard_map/pack_rows/pallas_call | solution.py:271
  6.5 19.3 %all-to-all-start = ((bf16[128,16,128]{2,1,0:T(8,128)(2,1)}), bf16[128,16,128]{2,1,0:T(8,128)(2,1)S(1)}, u32[]{:S(2)}, u32[]{:S(2)}) async-start(bf16[128,16,128]{2,1,0:T(8,128)(2,1)} %get-tuple-element.29), calls=%async_computation | async-start | bytes 1048576 | tf_op jit(solution)/shard_map/all_to_all | solution.py:277
  25.7 0.0 copy-start.8
  25.8 0.0 copy-done.6
  25.8 0.0 copy-done.7
  25.8 0.7 copy-done.8
  26.4 2.9 %row_scan.1 = (f32[256,384]{1,0:T(8,128)S(1)}, f32[32,384]{1,0:T(8,128)S(1)}, bf16[32,384]{1,0:T(8,128)(2,1)S(1)}, bf16[32,384]{1,0:T(8,128)(2,1)S(1)}, bf16[32,...) custom-call(bf16[256,384]{1,0:T(8,128)(2,1)S(1)} %get-tuple-element.30.xm_ref, ...), custom_call_target="tpu_custom_call" | custom-call | flops 4000000000 | bytes 1000000 | tf_op jit(solution)/shard_map/row_scan/pallas_call | solution.py:279
  29.3 20.8 %all-to-all-done.recv_ref = bf16[128,16,128]{2,1,0:T(8,128)(2,1)S(1)} async-done(((bf16[128,16,128]{2,1,0:T(8,128)(2,1)}), bf16[128,16,128]{2,1,0:T(8,128)(2,1)S(1)}, u32[]{:S(2)}, u32[]{:S(2)}) %all-to-all-start) | async-done | bytes 524320 | tf_op jit(solution)/shard_map/all_to_all | solution.py:277
  50.1 0.7 copy-done.9
  50.8 2.7 %col_pairs.1 = (bf16[4,96,128]{2,1,0:T(8,128)(2,1)}, bf16[12,128,128]{2,1,0:T(8,128)(2,1)S(1)}, bf16[3,128,256]{2,1,0:T(8,128)(2,1)S(1)}, bf16[3,128,256]{2,1,0:T(8,128)(2,1)S(1)}) custom-call(bf16[128,16,128]{2,1,0:T(8,128)(2,1)S(1)} %all-to-all-done.recv_ref, bf16[4,384]{1,0:T(4,128)(2,1)S(1)} %copy-done.9), custom_call_target="tpu_custom_call" | custom-call | flops 1000000000 | bytes 1000000 | tf_op jit(solution)/shard_map/col_pairs/pallas_call | solution.py:289
  53.5 3.3 %all-to-all-start.1 = ((bf16[4,96,128]{2,1,0:T(8,128)(2,1)}), bf16[4,96,128]{2,1,0:T(8,128)(2,1)S(1)}, u32[]{:S(2)}, u32[]{:S(2)}) async-start(bf16[4,96,128]{2,1,0:T(8,128)(2,1)} %get-tuple-element.34), calls=%async_computation.1 | async-start | bytes 196608 | tf_op jit(solution)/shard_map/all_to_all | solution.py:296
  56.8 1.5 %col_values.1 = (f32[128,8,128]{2,1,0:T(8,128)S(1)}, f32[16,128]{1,0:T(8,128)S(1)}) custom-call(bf16[12,128,128]{2,1,0:T(8,128)(2,1)S(1)} %get-tuple-element.35.a_ref, bf16[3,128,256]{2,1,0:T(8,128)(2,1)S(1)} %get-tuple-element.36.xt_ref, bf16[3,128,256]{2,1,0:T(8,128)(2,1)S(1)} %get-tuple-element.37.wt_ref), custom_call_target="tpu_custom_call" | custom-call | flops 2000000000 | bytes 1000000 | tf_op jit(solution)/shard_map/col_values/pallas_call | solution.py:298
  58.3 2.0 %all-to-all-done.1.hop_ref = bf16[4,96,128]{2,1,0:T(8,128)(2,1)S(1)} async-done(((bf16[4,96,128]{2,1,0:T(8,128)(2,1)}), bf16[4,96,128]{2,1,0:T(8,128)(2,1)S(1)}, u32[]{:S(2)}, u32[]{:S(2)}) %all-to-all-start.1) | async-done | bytes 98336 | tf_op jit(solution)/shard_map/all_to_all | solution.py:296
  60.4 0.8 pack_cols.1
  61.2 7.2 %all-to-all-start.2 = ((bf16[128,8,128]{2,1,0:T(8,128)(2,1)}), bf16[128,8,128]{2,1,0:T(8,128)(2,1)S(1)}, u32[]{:S(2)}, u32[]{:S(2)}) async-start(bf16[128,8,128]{2,1,0:T(8,128)(2,1)} %pack_cols.1), calls=%async_computation.2 | async-start | bytes 524288 | tf_op jit(solution)/shard_map/all_to_all | solution.py:307
  68.4 1.9 %collective-permute-start = (bf16[32,384]{1,0:T(8,128)(2,1)S(1)}, bf16[32,384]{1,0:T(8,128)(2,1)S(1)}, u32[]{:S(2)}, u32[]{:S(2)}) collective-permute-start(bf16[32,384]{1,0:T(8,128)(2,1)S(1)} %get-tuple-element.42), channel_id=1, source_target_pairs={{0,1},{1,2},{2,3},{3,0},{4,5},{5,6},{6,7},{7,4},{8,9},{9,10},{10,1... | collective-permute-start | bytes 73736 | tf_op jit(solution)/shard_map/ppermute | solution.py:286
  70.3 4.8 %collective-permute-start.1 = (bf16[32,384]{1,0:T(8,128)(2,1)S(1)}, bf16[32,384]{1,0:T(8,128)(2,1)S(1)}, u32[]{:S(2)}, u32[]{:S(2)}) collective-permute-start(bf16[32,384]{1,0:T(8,128)(2,1)S(1)} %get-tuple-element.43), channel_id=1, source_target_pairs={{0,2},{1,3},{2,0},{3,1},{4,6},{5,7},{6,4},{7,5},{8,10},{9,11},{10,... | collective-permute-start | bytes 73736 | tf_op jit(solution)/shard_map/ppermute | solution.py:286
  75.1 1.9 %collective-permute-start.2 = (bf16[32,384]{1,0:T(8,128)(2,1)S(1)}, bf16[32,384]{1,0:T(8,128)(2,1)S(1)}, u32[]{:S(2)}, u32[]{:S(2)}) collective-permute-start(bf16[32,384]{1,0:T(8,128)(2,1)S(1)} %get-tuple-element.44), channel_id=1, source_target_pairs={{0,3},{1,0},{2,1},{3,2},{4,7},{5,4},{6,5},{7,6},{8,11},{9,8},{10,9... | collective-permute-start | bytes 73736 | tf_op jit(solution)/shard_map/ppermute | solution.py:286
  77.0 0.0 collective-permute-done.r1_ref
  77.1 0.0 collective-permute-done.1.r2_ref
  77.1 3.6 %collective-permute-done.2.r3_ref = bf16[32,384]{1,0:T(8,128)(2,1)S(1)} collective-permute-done((bf16[32,384]{1,0:T(8,128)(2,1)S(1)}, bf16[32,384]{1,0:T(8,128)(2,1)S(1)}, u32[]{:S(2)}, u32[]{:S(2)}) %collective-permute-start.2) | collective-permute-done | bytes 24608 | tf_op jit(solution)/shard_map/ppermute | solution.py:286
  80.7 6.5 %all-to-all-done.2.back_ref = bf16[128,8,128]{2,1,0:T(8,128)(2,1)S(1)} async-done(((bf16[128,8,128]{2,1,0:T(8,128)(2,1)}), bf16[128,8,128]{2,1,0:T(8,128)(2,1)S(1)}, u32[]{:S(2)}, u32[]{:S(2)}) %all-to-all-start.2) | async-done | bytes 262176 | tf_op jit(solution)/shard_map/all_to_all | solution.py:307
  87.2 1.0 %join.1 = (bf16[256,384]{1,0:T(8,128)(2,1)}, bf16[16,384]{1,0:T(8,128)(2,1)}, bf16[16,384]{1,0:T(8,128)(2,1)}, bf16[16,384]{1,0:T(8,128)(2,1)}, bf16[16,384]{1,0:T(8,128)(2,1)}, /*index=5*/bf16[4,384]{1,0:T(4,128)(2,1)}) custom-call(bf16[128,8,128]{2,1,0:T(8,128)(2,1)S(1)} %all-to-all-done.2.back_ref, f32[256,384]{1,0:T(8,128)S(1)} %get-tuple-element.40.dx_ref, ...), custom_call_target="tpu_custom_call" | custom-call | flops 10000000 | bytes 1000000 | tf_op jit(solution)/shard_map/join/pallas_call | solution.py:309
  (6 shorter events, 0.0 us)
Async XLA Ops:
  0.6 0.7 copy-start.4
  0.6 0.7 copy-start.5
  1.3 0.9 %copy-start = (bf16[256,1,384]{2,0,1:T(8,128)(2,1)S(1)}, bf16[256,1,384]{2,0,1:T(8,128)(2,1)}, u32[]{:S(2)}) copy-start(bf16[256,1,384]{2,0,1:T(8,128)(2,1)} %param.9) | copy-start | bytes 589828
  2.2 0.9 %copy-start.1 = (bf16[256,1,384]{2,0,1:T(8,128)(2,1)S(1)}, bf16[256,1,384]{2,0,1:T(8,128)(2,1)}, u32[]{:S(2)}) copy-start(bf16[256,1,384]{2,0,1:T(8,128)(2,1)} %param.10) | copy-start | bytes 589828
  3.2 0.8 copy-start.2
  4.0 0.8 copy-start.3
  6.5 19.3 %copy-start.6 = (bf16[64,1,384]{2,0,1:T(8,128)(2,1)S(1)}, bf16[64,1,384]{2,0,1:T(8,128)(2,1)}, u32[]{:S(2)}) copy-start(bf16[64,1,384]{2,0,1:T(8,128)(2,1)} %param.11) | copy-start | bytes 147460
  6.5 19.3 %copy-start.7 = (bf16[64,1,384]{2,0,1:T(8,128)(2,1)S(1)}, bf16[64,1,384]{2,0,1:T(8,128)(2,1)}, u32[]{:S(2)}) copy-start(bf16[64,1,384]{2,0,1:T(8,128)(2,1)} %param.12) | copy-start | bytes 147460
  6.5 43.7 %all-to-all-start = ((bf16[128,16,128]{2,1,0:T(8,128)(2,1)}), bf16[128,16,128]{2,1,0:T(8,128)(2,1)S(1)}, u32[]{:S(2)}, u32[]{:S(2)}) async-start(bf16[128,16,128]{2,1,0:T(8,128)(2,1)} %get-tuple-element.29), calls=%async_computation | async-start | bytes 1048576 | tf_op jit(solution)/shard_map/all_to_all | solution.py:277
  25.7 0.7 copy-start.8
  50.1 0.7 copy-start.9
  53.5 6.8 %all-to-all-start.1 = ((bf16[4,96,128]{2,1,0:T(8,128)(2,1)}), bf16[4,96,128]{2,1,0:T(8,128)(2,1)S(1)}, u32[]{:S(2)}, u32[]{:S(2)}) async-start(bf16[4,96,128]{2,1,0:T(8,128)(2,1)} %get-tuple-element.34), calls=%async_computation.1 | async-start | bytes 196608 | tf_op jit(solution)/shard_map/all_to_all | solution.py:296
  61.2 26.0 %all-to-all-start.2 = ((bf16[128,8,128]{2,1,0:T(8,128)(2,1)}), bf16[128,8,128]{2,1,0:T(8,128)(2,1)S(1)}, u32[]{:S(2)}, u32[]{:S(2)}) async-start(bf16[128,8,128]{2,1,0:T(8,128)(2,1)} %pack_cols.1), calls=%async_computation.2 | async-start | bytes 524288 | tf_op jit(solution)/shard_map/all_to_all | solution.py:307
  68.4 8.7 %collective-permute-start = (bf16[32,384]{1,0:T(8,128)(2,1)S(1)}, bf16[32,384]{1,0:T(8,128)(2,1)S(1)}, u32[]{:S(2)}, u32[]{:S(2)}) collective-permute-start(bf16[32,384]{1,0:T(8,128)(2,1)S(1)} %get-tuple-element.42), channel_id=1, source_target_pairs={{0,1},{1,2},{2,3},{3,0},{4,5},{5,6},{6,7},{7,4},{8,9},{9,10},{10,1... | collective-permute-start | bytes 73736 | tf_op jit(solution)/shard_map/ppermute | solution.py:286
  70.3 6.7 %collective-permute-start.1 = (bf16[32,384]{1,0:T(8,128)(2,1)S(1)}, bf16[32,384]{1,0:T(8,128)(2,1)S(1)}, u32[]{:S(2)}, u32[]{:S(2)}) collective-permute-start(bf16[32,384]{1,0:T(8,128)(2,1)S(1)} %get-tuple-element.43), channel_id=1, source_target_pairs={{0,2},{1,3},{2,0},{3,1},{4,6},{5,7},{6,4},{7,5},{8,10},{9,11},{10,... | collective-permute-start | bytes 73736 | tf_op jit(solution)/shard_map/ppermute | solution.py:286
  75.1 5.6 %collective-permute-start.2 = (bf16[32,384]{1,0:T(8,128)(2,1)S(1)}, bf16[32,384]{1,0:T(8,128)(2,1)S(1)}, u32[]{:S(2)}, u32[]{:S(2)}) collective-permute-start(bf16[32,384]{1,0:T(8,128)(2,1)S(1)} %get-tuple-element.44), channel_id=1, source_target_pairs={{0,3},{1,0},{2,1},{3,2},{4,7},{5,4},{6,5},{7,6},{8,11},{9,8},{10,9... | collective-permute-start | bytes 73736 | tf_op jit(solution)/shard_map/ppermute | solution.py:286
where the time goes:
time: 88.9 us; the launch traced here: 88.2 us
  starting transfers between devices  38.4 us (43%)
  waiting for transfers between devices  32.9 us (37%)
  Pallas kernels  10.7 us (12%)
  local copies, waits for them, and re-layouts  5.47 us (6%)
    all_to_all x1, waiting for transfers between devices, body(): recv = lax.all_to_all(send, 'rows', split_axis=0, concat_axis=0, tiled=True)  20.8 us
    all_to_all x1, starting transfers between devices, body(): recv = lax.all_to_all(send, 'rows', split_axis=0, concat_axis=0, tiled=True)  19.3 us
    ppermute x3, starting transfers between devices, body(): lax.ppermute(part, 'heads', [(i, (i + shift) % 4) for i in range(4)])  8.63 us
    all_to_all x1, starting transfers between devices, body(): lax.all_to_all(packed, 'rows', split_axis=0, concat_axis=0, tiled=True)  7.19 us
    all_to_all x1, waiting for transfers between devices, body(): lax.all_to_all(packed, 'rows', split_axis=0, concat_axis=0, tiled=True)  6.52 us
    unnamed x20, local copies, waits for them, and re-layouts  5.47 us
    ppermute x3, waiting for transfers between devices, body(): lax.ppermute(part, 'heads', [(i, (i + shift) % 4) for i in range(4)])  3.62 us
    all_to_all x1, starting transfers between devices, body(): lax.all_to_all(hop, 'heads', split_axis=0, concat_axis=0, tiled=True)  3.29 us
  transfers between devices with their start and end apart: 6, of which 4 were waited for; matrix products, arithmetic and copies ran while one was open for 0% of the time, Pallas kernels for 5%

commit v1 on v0

--- a/solution.py
+++ b/solution.py
@@ -47,33 +47,59 @@
     return nn(rows, spread)[0:1]
 
 
-def prep_kernel(x_ref, w_ref, u_ref, v_ref, a_ref, tis_ref, send_ref, xm_ref, wm_ref, wt_ref, scr):
+def prep_kernel(x_any, w_any, u_any, v_any, a_any, tis_any, send_any, x_ref, w_ref, u_ref, v_ref, a_ref, tis_ref, send_ref, scr, sems, out_sems):
     n = x_ref.shape[1]
     blocks = n // L
+    halves = x_ref.shape[0] // L
+    per = 2 * halves + 1
+    heads = a_ref.shape[0]
+    pairs = [(tis_any, tis_ref), (u_any, u_ref), (v_any, v_ref), (a_any, a_ref)]
+    for whole, mine in ((x_any, x_ref), (w_any, w_ref)):
+        pairs += [(whole.at[pl.ds(r * L, L)], mine.at[pl.ds(r * L, L)]) for r in range(halves)]
+    copies = [pltpu.make_async_copy(src, dst, sems.at[i]) for i, (src, dst) in enumerate(pairs)]
+    for copy in copies:
+        copy.start()
+    for copy in copies[:4]:
+        copy.wait()
+    keep = keep_of(tis_ref[...], n)
+    for k in range(blocks):
+        at = pl.ds(k * L, L)
+        uv = jnp.concatenate([u_ref[:, at].astype(F32), v_ref[:, at].astype(F32)], axis=0)
+        scr[:, per * k + 2 * halves, :] = uv.T
+    a = [a_ref[:, pl.ds(k * L, L)].astype(F32) for k in range(blocks)]
+    a.append(jnp.zeros((L - heads * blocks, L), F32))
+    scr[:, per * blocks, :] = jnp.concatenate(a, axis=0).T
+    for o, ref in ((0, x_ref), (halves, w_ref)):
+        for r in range(halves):
+            copies[4 + o + r].wait()
+            for k in range(blocks):
+                at = pl.ds(k * L, L)
+                part = ref[pl.ds(r * L, L), at].astype(F32) * keep[:, k * L : (k + 1) * L]
+                scr[:, per * k + o + r, :] = part.T
+    send_out(scr, send_ref, send_any, out_sems)
+
+
+def send_out(src, mid, dst, sems):
+    pieces = sems.shape[0]
+    size = src.shape[0] // pieces
+    copies = []
+    for i in range(pieces):
+        at = pl.ds(i * size, size)
+        mid[at] = src[at].astype(mid.dtype)
+        copies.append(pltpu.make_async_copy(mid.at[at], dst.at[at], sems.at[i]))
+        copies[-1].start()
+    for copy in copies:
+        copy.wait()
+
+
+def row_kernel(x_ref, w_ref, tis_ref, u_ref, v_ref, a_ref, dx_ref, d0_ref, d1_ref, d2_ref, d3_ref, da_ref, y_ref, duv_ref, xm_ref, wm_ref, wt_ref):
+    n = x_ref.shape[1]
     keep = keep_of(tis_ref[...], n).astype(BF16)
     xm_ref[...] = x_ref[...] * keep
     wm_ref[...] = w_ref[...] * keep
-    halves = x_ref.shape[0] // L
-    per = 2 * halves + 1
-    for k in range(blocks):
-        at = pl.ds(k * L, L)
-        for r in range(halves):
-            ch = pl.ds(r * L, L)
-            scr[:, per * k + r, :] = xm_ref[ch, at].astype(F32).T
-            wt = wm_ref[ch, at].astype(F32).T
-            scr[:, per * k + halves + r, :] = wt
-            wt_ref[at, ch] = wt.astype(BF16)
-        uv = jnp.concatenate([u_ref[:, at].astype(F32), v_ref[:, at].astype(F32)], axis=0)
-        scr[:, per * k + 2 * halves, :] = uv.T
-    heads = a_ref.shape[0]
-    a = [a_ref[:, pl.ds(k * L, L)].astype(F32) for k in range(blocks)]
-    a.append(jnp.zeros((L - heads * blocks, L), F32))
-    scr[:, per * blocks, :] = jnp.concatenate(a, axis=0).T
-    send_ref[...] = scr[...].astype(BF16)
-
-
-def row_kernel(xm_ref, wm_ref, wt_ref, u_ref, v_ref, a_ref, dx_ref, d0_ref, d1_ref, d2_ref, d3_ref, da_ref, y_ref, duv_ref):
-    n = xm_ref.shape[1]
+    for b in range(n // L):
+        for r in range(x_ref.shape[0] // L):
+            wt_ref[pl.ds(b * L, L), pl.ds(r * L, L)] = wm_ref[pl.ds(r * L, L), pl.ds(b * L, L)].astype(F32).T.astype(BF16)
     blocks = n // L
     heads = a_ref.shape[0]
     nstate = u_ref.shape[0]
@@ -144,7 +170,7 @@
         da_ref[:, at] = da.astype(BF16)
 
 
-def col_pair_kernel(recv_ref, after_ref, hop_ref, a_ref, xt_ref, wt_ref, scr, *, blocks, heads):
+def col_pair_kernel(recv_ref, after0_ref, after1_ref, hop_any, a_ref, xt_ref, wt_ref, scr, d_ref, hop_ref, sems, *, blocks, heads):
     scr[...] = recv_ref[...].astype(F32)
     halves = heads // 2
     per = 2 * halves + 1
@@ -154,31 +180,39 @@
     later = i0 <= i1
     gcol = tn(tri, scr[:, per * blocks, :].astype(BF16))
     grow = gcol.T
+    quarter = HD // 4
+    copies = []
     for k in range(blocks):
         for r in range(halves):
             xt_ref[k, :, pl.ds(r * L, L)] = scr[:, per * k + r, :].astype(BF16)
             wt_ref[k, :, pl.ds(r * L, L)] = scr[:, per * k + halves + r, :].astype(BF16)
-        uvt = scr[:, per * k + 2 * halves, :]
-        uv = uvt.T.astype(BF16)
+        uv = scr[:, per * k + 2 * halves, :].T.astype(BF16)
         u, v = uv[:HD], uv[HD:]
-        s = nn(uvt[:, :HD].astype(BF16), v)
         q = None
         for h in range(heads):
             ch = pl.ds(h * HD, HD)
             c = heads * k + h
             d = jnp.exp(jnp.minimum(grow[c : c + 1, :] - gcol[:, c : c + 1], 0.0))
             d = jnp.where(later, d, 0.0)
-            m = nt(xt_ref[k, :, ch], wt_ref[k, :, ch])
-            dm = d * m
+            d_ref[c] = d
+            dm = d * nt(xt_ref[k, :, ch], wt_ref[k, :, ch])
             q = dm if q is None else q + dm
-            a_ref[c] = (d * s).astype(BF16)
         qb = q.astype(BF16)
         du = nt(v, qb).astype(BF16)
         dv = nn(u, qb).astype(BF16)
-        quarter = HD // 4
+        at = pl.ds(2 * quarter * k, 2 * quarter)
         for p in range(4):
             hop_ref[p, pl.ds(2 * quarter * k, quarter), :] = du[quarter * p : quarter * (p + 1)]
             hop_ref[p, pl.ds(2 * quarter * k + quarter, quarter), :] = dv[quarter * p : quarter * (p + 1)]
+        copies.append(pltpu.make_async_copy(hop_ref.at[:, at], hop_any.at[:, at], sems.at[k]))
+        copies[-1].start()
+    for k in range(blocks):
+        uvt = scr[:, per * k + 2 * halves, :]
+        s = nn(uvt[:, :HD].astype(BF16), uvt.T[HD:].astype(BF16))
+        for h in range(heads):
+            a_ref[heads * k + h] = (d_ref[heads * k + h] * s).astype(BF16)
+    for copy in copies:
+        copy.wait()
 
 
 def col_value_kernel(a_ref, xt_ref, wt_ref, ret_ref, da_ref, y_ref, dx_ref, *, blocks, heads):
@@ -208,7 +242,7 @@
     da_ref[...] = nn(hi, suffix) + nn(mid, suffix) + nn(lo, suffix)
 
 
-def pack_kernel(hop_ref, ret_ref, da_ref, out_ref, scr, *, used):
+def pack_kernel(hop_ref, ret_ref, da_ref, out_any, scr, out_ref, sems, *, used):
     total = hop_ref[0].astype(F32)
     for p in range(1, 4):
         total += hop_ref[p].astype(F32)
@@ -217,7 +251,7 @@
     scr[...] = ret_ref[...]
     scr[:, used, :] = jnp.concatenate(small, axis=0).T
     scr[:, used + 1, :] = jnp.zeros((L, L), F32)
-    out_ref[...] = scr[...].astype(BF16)
+    send_out(scr, out_ref, out_any, sems)
 
 
 def final_kernel(back_ref, dx_ref, tis_ref, r0_ref, r1_ref, r2_ref, r3_ref, gx_ref, iu_ref, iv_ref, cu_ref, cv_ref, da_ref, scr, *, heads):
@@ -246,15 +280,17 @@
     iv_ref[...] = row[quarter:].astype(BF16)
 
 
-def call(kernel, outs, scratch, flops, moved, name, in_specs=None):
-    more = {} if in_specs is None else {"in_specs": in_specs}
+def call(kernel, outs, scratch, flops, name, limit=32, ins=None):
+    place = lambda far: pl.BlockSpec(memory_space=pl.ANY if far else pltpu.VMEM)
+    more = {} if ins is None else {"in_specs": [place(far) for far in ins]}
     return pl.pallas_call(
         kernel,
         **more,
-        out_shape=[jax.ShapeDtypeStruct(s, d) for s, d in outs],
-        scratch_shapes=[pltpu.VMEM(s, F32) for s in scratch],
-        compiler_params=pltpu.CompilerParams(vmem_limit_bytes=32 * 2**20),
-        cost_estimate=pl.CostEstimate(flops=flops, bytes_accessed=moved, transcendentals=0),
+        out_shape=[jax.ShapeDtypeStruct(o[0], o[1]) for o in outs],
+        out_specs=[place(len(o) > 2) for o in outs],
+        scratch_shapes=scratch,
+        compiler_params=pltpu.CompilerParams(vmem_limit_bytes=limit * 2**20),
+        cost_estimate=pl.CostEstimate(flops=flops, bytes_accessed=10**6, transcendentals=0),
         name=name,
     )
 
@@ -263,54 +299,65 @@
     heads = decay_row.shape[0]
     chan, _, n = features.shape
     nstate = inject_row.shape[0]
+    quarter = nstate // 4
     blocks = n // L
     flat = lambda x: x.reshape(x.shape[0], n)
+    vm, dma = pltpu.VMEM, pltpu.SemaphoreType.DMA
     x, w = flat(features), flat(cotangent)
     per = 2 * chan // L + 1
     rows_out = per * blocks + 1
-    send, xm, wm, wt = call(
+    tile = (L, rows_out, L)
+    (send,) = call(
         prep_kernel,
-        [((L, rows_out, L), BF16), ((chan, n), BF16), ((chan, n), BF16), ((n, chan), BF16)],
-        [(L, rows_out, L)],
-        10**7, 10**6, "pack_rows",
+        [(tile, BF16, "far")],
+        [
+            vm((chan, n), BF16), vm((chan, n), BF16), vm((nstate, n), BF16), vm((nstate, n), BF16),
+            vm((heads, n), BF16), vm(tissue.shape, jnp.int32), vm(tile, BF16), vm(tile, F32),
+            dma((4 + 2 * chan // L,)), dma((8,)),
+        ],
+        10**7, "pack_rows", 60, [True] * 6,
     )(x, w, flat(inject_col), flat(readout_col), flat(decay_col), tissue)
     recv = lax.all_to_all(send, "rows", split_axis=0, concat_axis=0, tiled=True)
-    share = (nstate // 2, n)
+    share = (2 * quarter, n)
     dx_row, mine, *theirs, da_row = call(
         row_kernel,
         [((chan, n), F32), (share, F32), (share, BF16), (share, BF16), (share, BF16), ((heads, n), BF16)],
-        [(chan, n), (2 * nstate, n)],
-        4 * 10**9, 10**6, "row_scan",
-    )(xm, wm, wt, flat(inject_row), flat(readout_row), flat(decay_row))
+        [vm((chan, n), F32), vm((2 * nstate, n), F32), vm((chan, n), BF16), vm((chan, n), BF16), vm((n, chan), BF16)],
+        4 * 10**9, "row_scan",
+    )(x, w, tissue, flat(inject_row), flat(readout_row), flat(decay_row))
     shares = [
         lax.ppermute(part, "heads", [(i, (i + shift) % 4) for i in range(4)]) for shift, part in enumerate(theirs, 1)
     ]
     sizes = dict(blocks=blocks, heads=heads)
+    hop_shape = (4, 2 * quarter * blocks, L)
+    per_col = (blocks, L, chan)
     hop, weights, xt, wtc = call(
         partial(col_pair_kernel, **sizes),
-        [((4, nstate // 2 * blocks, L), BF16), ((blocks * heads, L, L), BF16), ((blocks, L, chan), BF16), ((blocks, L, chan), BF16)],
-        [(L, rows_out, L)],
-        10**9, 10**6, "col_pairs",
-        [pl.BlockSpec(memory_space=pltpu.VMEM), pl.BlockSpec(memory_space=pl.ANY)],
-    )(recv, da_row)
+        [(hop_shape, BF16, "far"), ((blocks * heads, L, L), BF16), (per_col, BF16), (per_col, BF16)],
+        [vm(tile, F32), vm((blocks * heads, L, L), F32), vm(hop_shape, BF16), dma((blocks,))],
+        10**9, "col_pairs",
+    )(recv, shares[0], shares[2])
     hopped = lax.all_to_all(hop, "heads", split_axis=0, concat_axis=0, tiled=True)
     used = blocks * heads // 2
+    back_tile = (L, used + 2, L)
     ret, da_col = call(
         partial(col_value_kernel, **sizes),
-        [((L, used + 2, L), F32), ((16, L), F32)],
-        [(L, chan), (L, chan)],
-        2 * 10**9, 10**6, "col_values",
+        [(back_tile, F32), ((16, L), F32)],
+        [vm((L, chan), F32), vm((L, chan), F32)],
+        2 * 10**9, "col_values",
     )(weights, xt, wtc)
     (packed,) = call(
-        partial(pack_kernel, used=used), [((L, used + 2, L), BF16)], [(L, used + 2, L)], 10**7, 10**6, "pack_cols"
+        partial(pack_kernel, used=used),
+        [(back_tile, BF16, "far")],
+        [vm(back_tile, F32), vm(back_tile, BF16), dma((4,))],
+        10**7, "pack_cols",
     )(hopped, ret, da_col)
     back = lax.all_to_all(packed, "rows", split_axis=0, concat_axis=0, tiled=True)
-    quarter = nstate // 4
     gx, iu, iv, cu, cv, da = call(
         partial(final_kernel, heads=heads),
         [((chan, n), BF16)] + [((quarter, n), BF16)] * 4 + [((heads, n), BF16)],
-        [(L, used + 2, L)],
-        10**7, 10**6, "join",
+        [vm(back_tile, F32)],
+        10**7, "join",
     )(back, dx_row, tissue, mine, *shares)
     wide = lambda x: x.reshape(x.shape[0], 1, n)
     return wide(gx), wide(iu), wide(iv), wide(cu), wide(cv), wide(da_row), wide(da)

time: 88.9 us -> 87.4 us (0.983)
  local copies, waits for them, and re-layouts: 5.47 us -> 0.66 us
  waiting for transfers between devices: 32.9 us -> 34.1 us
  Pallas kernels: 10.7 us -> 11.9 us
  starting transfers between devices: 38.4 us -> 39.5 us
    all_to_all x1, waiting for transfers between devices: 20.8 us -> 12.8 us  [body(): recv = lax.all_to_all(send, 'rows', split_axis=0, concat_axis=0, tiled=True)]
    all_to_all x1, waiting for transfers between devices: 6.52 us -> 13.1 us  [body(): lax.all_to_all(packed, 'rows', split_axis=0, concat_axis=0, tiled=True)]
    unnamed x20 -> x12, local copies, waits for them, and re-layouts: 5.47 us -> 0.66 us
    ppermute x3, waiting for transfers between devices: 3.62 us -> 6.16 us  [body(): lax.ppermute(part, 'heads', [(i, (i + shift) % 4) for i in range(4)])]
    all_to_all x1, starting transfers between devices: 7.19 us -> 9.49 us  [body(): lax.all_to_all(packed, 'rows', split_axis=0, concat_axis=0, tiled=True)]
    ppermute x3, starting transfers between devices: 8.63 us -> 7.43 us  [body(): lax.ppermute(part, 'heads', [(i, (i + shift) % 4) for i in range(4)])]
  transfers between devices with their start and end apart: 6 -> 6, of which waited for: 4 -> 5; matrix products, arithmetic and copies ran while one was open for 0% -> 0% of each run, Pallas kernels for 5% -> 5%
where the time goes in v1:
time: 87.4 us; the launch traced here: 87 us
  starting transfers between devices  39.5 us (45%)
  waiting for transfers between devices  34.1 us (39%)
  Pallas kernels  11.9 us (14%)
    all_to_all x1, starting transfers between devices, body(): recv = lax.all_to_all(send, 'rows', split_axis=0, concat_axis=0, tiled=True)  19.3 us
    all_to_all x1, waiting for transfers between devices, body(): lax.all_to_all(packed, 'rows', split_axis=0, concat_axis=0, tiled=True)  13.1 us
    all_to_all x1, waiting for transfers between devices, body(): recv = lax.all_to_all(send, 'rows', split_axis=0, concat_axis=0, tiled=True)  12.8 us
    all_to_all x1, starting transfers between devices, body(): lax.all_to_all(packed, 'rows', split_axis=0, concat_axis=0, tiled=True)  9.49 us
    ppermute x3, starting transfers between devices, body(): lax.ppermute(part, 'heads', [(i, (i + shift) % 4) for i in range(4)])  7.43 us
    ppermute x3, waiting for transfers between devices, body(): lax.ppermute(part, 'heads', [(i, (i + shift) % 4) for i in range(4)])  6.16 us
    all_to_all x1, starting transfers between devices, body(): lax.all_to_all(hop, 'heads', split_axis=0, concat_axis=0, tiled=True)  3.31 us
    pallas_call x1, Pallas kernels, body(): call(row_kernel, [((chan, n), F32), (share, F32), (share, BF16), (share,...  3.27 us
  transfers between devices with their start and end apart: 6, of which 5 were waited for; matrix products, arithmetic and copies ran while one was open for 0% of the time, Pallas kernels for 5%

profile of v1, /device:TPU:9, one launch (start us, length us, event | category | flops | bytes accessed | tf_op | source)
XLA Modules:
  0.0 87.0 jit_solution(6355662471495723476)
XLA Ops:
  0.6 2.7 %pack_rows.1 = bf16[128,16,128]{2,1,0:T(8,128)(2,1)} custom-call(bf16[256,384]{1,0:T(8,128)(2,1)} %bitcast.15, bf16[256,384]{1,0:T(8,128)(2,1)} %bitcast.17, bf16[64,384]{1,0:T(8,128)(2,1)} %bitcast.22, bf16[64,384]{1,0:T(8,128)(2,1)} %bitcast.23, bf16[4,384]{1,0:T(4,128)(2,1)} %bitcast.24, s32[1,24]{1,0:T(1,128)} %tis_ref.3), custom_call_target="tpu_custom_call" | custom-call | flops 10000000 | bytes 1000000 | tf_op jit(solution)/shard_map/pack_rows/pallas_call | solution.py:310
  3.3 0.0 copy-start
  3.3 0.0 copy-start.1
  3.3 0.0 copy-start.3
  3.4 0.0 copy-start.4
  3.4 19.3 %all-to-all-start = ((bf16[128,16,128]{2,1,0:T(8,128)(2,1)}), bf16[128,16,128]{2,1,0:T(8,128)(2,1)S(1)}, u32[]{:S(2)}, u32[]{:S(2)}) async-start(bf16[128,16,128]{2,1,0:T(8,128)(2,1)} %pack_rows.1), calls=%async_computation | async-start | bytes 1048576 | tf_op jit(solution)/shard_map/all_to_all | solution.py:320
  22.7 0.0 copy-start.5
  22.7 0.0 copy-start.2
  22.7 0.0 copy-done
  22.7 0.0 copy-done.1
  22.7 0.0 copy-done.3
  22.7 0.0 copy-done.4
  22.7 0.6 copy-done.5
  23.4 0.0 copy-done.2
  23.4 3.3 %row_scan.1 = (f32[256,384]{1,0:T(8,128)S(1)}, f32[32,384]{1,0:T(8,128)S(1)}, bf16[32,384]{1,0:T(8,128)(2,1)S(1)}, bf16[32,384]{1,0:T(8,128)(2,1)S(1)}, bf16[32,...) custom-call(bf16[256,384]{1,0:T(8,128)(2,1)S(1)} %bitcast.16, bf16[256,384]{1,0:T(8,128)(2,1)S(1)} %bitcast.18, ...), custom_call_target="tpu_custom_call" | custom-call | flops 4000000000 | bytes 1000000 | tf_op jit(solution)/shard_map/row_scan/pallas_call | solution.py:322
  26.6 2.3 %collective-permute-start = (bf16[32,384]{1,0:T(8,128)(2,1)S(1)}, bf16[32,384]{1,0:T(8,128)(2,1)S(1)}, u32[]{:S(2)}, u32[]{:S(2)}) collective-permute-start(bf16[32,384]{1,0:T(8,128)(2,1)S(1)} %get-tuple-element.25), channel_id=1, source_target_pairs={{0,1},{1,2},{2,3},{3,0},{4,5},{5,6},{6,7},{7,4},{8,9},{9,10},{10,1... | collective-permute-start | bytes 73736 | tf_op jit(solution)/shard_map/ppermute | solution.py:329
  28.9 3.0 %collective-permute-start.1 = (bf16[32,384]{1,0:T(8,128)(2,1)S(1)}, bf16[32,384]{1,0:T(8,128)(2,1)S(1)}, u32[]{:S(2)}, u32[]{:S(2)}) collective-permute-start(bf16[32,384]{1,0:T(8,128)(2,1)S(1)} %get-tuple-element.26), channel_id=1, source_target_pairs={{0,3},{1,0},{2,1},{3,2},{4,7},{5,4},{6,5},{7,6},{8,11},{9,8},{10,9... | collective-permute-start | bytes 73736 | tf_op jit(solution)/shard_map/ppermute | solution.py:329
  31.9 0.0 collective-permute-done.after0_ref.r1_ref
  31.9 2.6 %collective-permute-done.1.after1_ref.r3_ref = bf16[32,384]{1,0:T(8,128)(2,1)S(1)} collective-permute-done((bf16[32,384]{1,0:T(8,128)(2,1)S(1)}, bf16[32,384]{1,0:T(8,128)(2,1)S(1)}, u32[]{:S(2)}, u32[]{:S(2)}) %collective-permute-start.1) | collective-permute-done | bytes 24608 | tf_op jit(solution)/shard_map/ppermute | solution.py:329
  34.5 12.8 %all-to-all-done.recv_ref = bf16[128,16,128]{2,1,0:T(8,128)(2,1)S(1)} async-done(((bf16[128,16,128]{2,1,0:T(8,128)(2,1)}), bf16[128,16,128]{2,1,0:T(8,128)(2,1)S(1)}, u32[]{:S(2)}, u32[]{:S(2)}) %all-to-all-start) | async-done | bytes 524320 | tf_op jit(solution)/shard_map/all_to_all | solution.py:320
  47.3 2.6 %col_pairs.1 = (bf16[4,96,128]{2,1,0:T(8,128)(2,1)}, bf16[12,128,128]{2,1,0:T(8,128)(2,1)S(1)}, bf16[3,128,256]{2,1,0:T(8,128)(2,1)S(1)}, bf16[3,128,256]{2,1,0:T(8,128)(2,1)S(1)}) custom-call(bf16[128,16,128]{2,1,0:T(8,128)(2,1)S(1)} %all-to-all-done.recv_ref, bf16[32,384]{1,0:T(8,128)(2,1)S(1)} %collective-permute-done.after0_ref.r1_ref, ...), custom_call_target="tpu_custom_call" | custom-call | flops 1000000000 | bytes 1000000 | tf_op jit(solution)/shard_map/col_pairs/pallas_call | solution.py:334
  49.9 3.3 %all-to-all-start.1 = ((bf16[4,96,128]{2,1,0:T(8,128)(2,1)}), bf16[4,96,128]{2,1,0:T(8,128)(2,1)S(1)}, u32[]{:S(2)}, u32[]{:S(2)}) async-start(bf16[4,96,128]{2,1,0:T(8,128)(2,1)} %get-tuple-element.27), calls=%async_computation.1 | async-start | bytes 196608 | tf_op jit(solution)/shard_map/all_to_all | solution.py:340
  53.2 1.5 %col_values.1 = (f32[128,8,128]{2,1,0:T(8,128)S(1)}, f32[16,128]{1,0:T(8,128)S(1)}) custom-call(bf16[12,128,128]{2,1,0:T(8,128)(2,1)S(1)} %get-tuple-element.28.a_ref, bf16[3,128,256]{2,1,0:T(8,128)(2,1)S(1)} %get-tuple-element.29.xt_ref, bf16[3,128,256]{2,1,0:T(8,128)(2,1)S(1)} %get-tuple-element.30.wt_ref), custom_call_target="tpu_custom_call" | custom-call | flops 2000000000 | bytes 1000000 | tf_op jit(solution)/shard_map/col_values/pallas_call | solution.py:343
  54.7 2.0 %all-to-all-done.1.hop_ref = bf16[4,96,128]{2,1,0:T(8,128)(2,1)S(1)} async-done(((bf16[4,96,128]{2,1,0:T(8,128)(2,1)}), bf16[4,96,128]{2,1,0:T(8,128)(2,1)S(1)}, u32[]{:S(2)}, u32[]{:S(2)}) %all-to-all-start.1) | async-done | bytes 98336 | tf_op jit(solution)/shard_map/all_to_all | solution.py:340
  56.7 0.8 pack_cols.1
  57.5 9.5 %all-to-all-start.2 = ((bf16[128,8,128]{2,1,0:T(8,128)(2,1)}), bf16[128,8,128]{2,1,0:T(8,128)(2,1)S(1)}, u32[]{:S(2)}, u32[]{:S(2)}) async-start(bf16[128,8,128]{2,1,0:T(8,128)(2,1)} %pack_cols.1), calls=%async_computation.2 | async-start | bytes 524288 | tf_op jit(solution)/shard_map/all_to_all | solution.py:355
  67.0 2.2 %collective-permute-start.2 = (bf16[32,384]{1,0:T(8,128)(2,1)S(1)}, bf16[32,384]{1,0:T(8,128)(2,1)S(1)}, u32[]{:S(2)}, u32[]{:S(2)}) collective-permute-start(bf16[32,384]{1,0:T(8,128)(2,1)S(1)} %get-tuple-element.35), channel_id=1, source_target_pairs={{0,2},{1,3},{2,0},{3,1},{4,6},{5,7},{6,4},{7,5},{8,10},{9,11},{10,... | collective-permute-start | bytes 73736 | tf_op jit(solution)/shard_map/ppermute | solution.py:329
  69.2 3.6 %collective-permute-done.2.r2_ref = bf16[32,384]{1,0:T(8,128)(2,1)S(1)} collective-permute-done((bf16[32,384]{1,0:T(8,128)(2,1)S(1)}, bf16[32,384]{1,0:T(8,128)(2,1)S(1)}, u32[]{:S(2)}, u32[]{:S(2)}) %collective-permute-start.2) | collective-permute-done | bytes 24608 | tf_op jit(solution)/shard_map/ppermute | solution.py:329
  72.8 13.1 %all-to-all-done.2.back_ref = bf16[128,8,128]{2,1,0:T(8,128)(2,1)S(1)} async-done(((bf16[128,8,128]{2,1,0:T(8,128)(2,1)}), bf16[128,8,128]{2,1,0:T(8,128)(2,1)S(1)}, u32[]{:S(2)}, u32[]{:S(2)}) %all-to-all-start.2) | async-done | bytes 262176 | tf_op jit(solution)/shard_map/all_to_all | solution.py:355
  85.9 1.0 %join.1 = (bf16[256,384]{1,0:T(8,128)(2,1)}, bf16[16,384]{1,0:T(8,128)(2,1)}, bf16[16,384]{1,0:T(8,128)(2,1)}, bf16[16,384]{1,0:T(8,128)(2,1)}, bf16[16,384]{1,0:T(8,128)(2,1)}, /*index=5*/bf16[4,384]{1,0:T(4,128)(2,1)}) custom-call(bf16[128,8,128]{2,1,0:T(8,128)(2,1)S(1)} %all-to-all-done.2.back_ref, f32[256,384]{1,0:T(8,128)S(1)} %get-tuple-element.33.dx_ref, ...), custom_call_target="tpu_custom_call" | custom-call | flops 10000000 | bytes 1000000 | tf_op jit(solution)/shard_map/join/pallas_call | solution.py:356
Async XLA Ops:
  3.3 19.4 %copy-start = (bf16[256,1,384]{2,0,1:T(8,128)(2,1)S(1)}, bf16[256,1,384]{2,0,1:T(8,128)(2,1)}, u32[]{:S(2)}) copy-start(bf16[256,1,384]{2,0,1:T(8,128)(2,1)} %param.9) | copy-start | bytes 589828
  3.3 19.4 %copy-start.1 = (bf16[256,1,384]{2,0,1:T(8,128)(2,1)S(1)}, bf16[256,1,384]{2,0,1:T(8,128)(2,1)}, u32[]{:S(2)}) copy-start(bf16[256,1,384]{2,0,1:T(8,128)(2,1)} %param.10) | copy-start | bytes 589828
  3.3 19.4 %copy-start.3 = (bf16[64,1,384]{2,0,1:T(8,128)(2,1)S(1)}, bf16[64,1,384]{2,0,1:T(8,128)(2,1)}, u32[]{:S(2)}) copy-start(bf16[64,1,384]{2,0,1:T(8,128)(2,1)} %param.11) | copy-start | bytes 147460
  3.4 19.4 %copy-start.4 = (bf16[64,1,384]{2,0,1:T(8,128)(2,1)S(1)}, bf16[64,1,384]{2,0,1:T(8,128)(2,1)}, u32[]{:S(2)}) copy-start(bf16[64,1,384]{2,0,1:T(8,128)(2,1)} %param.12) | copy-start | bytes 147460
  3.4 43.9 %all-to-all-start = ((bf16[128,16,128]{2,1,0:T(8,128)(2,1)}), bf16[128,16,128]{2,1,0:T(8,128)(2,1)S(1)}, u32[]{:S(2)}, u32[]{:S(2)}) async-start(bf16[128,16,128]{2,1,0:T(8,128)(2,1)} %pack_rows.1), calls=%async_computation | async-start | bytes 1048576 | tf_op jit(solution)/shard_map/all_to_all | solution.py:320
  22.7 0.7 copy-start.5
  22.7 0.7 copy-start.2
  26.6 5.3 %collective-permute-start = (bf16[32,384]{1,0:T(8,128)(2,1)S(1)}, bf16[32,384]{1,0:T(8,128)(2,1)S(1)}, u32[]{:S(2)}, u32[]{:S(2)}) collective-permute-start(bf16[32,384]{1,0:T(8,128)(2,1)S(1)} %get-tuple-element.25), channel_id=1, source_target_pairs={{0,1},{1,2},{2,3},{3,0},{4,5},{5,6},{6,7},{7,4},{8,9},{9,10},{10,1... | collective-permute-start | bytes 73736 | tf_op jit(solution)/shard_map/ppermute | solution.py:329
  28.9 5.5 %collective-permute-start.1 = (bf16[32,384]{1,0:T(8,128)(2,1)S(1)}, bf16[32,384]{1,0:T(8,128)(2,1)S(1)}, u32[]{:S(2)}, u32[]{:S(2)}) collective-permute-start(bf16[32,384]{1,0:T(8,128)(2,1)S(1)} %get-tuple-element.26), channel_id=1, source_target_pairs={{0,3},{1,0},{2,1},{3,2},{4,7},{5,4},{6,5},{7,6},{8,11},{9,8},{10,9... | collective-permute-start | bytes 73736 | tf_op jit(solution)/shard_map/ppermute | solution.py:329
  49.9 6.8 %all-to-all-start.1 = ((bf16[4,96,128]{2,1,0:T(8,128)(2,1)}), bf16[4,96,128]{2,1,0:T(8,128)(2,1)S(1)}, u32[]{:S(2)}, u32[]{:S(2)}) async-start(bf16[4,96,128]{2,1,0:T(8,128)(2,1)} %get-tuple-element.27), calls=%async_computation.1 | async-start | bytes 196608 | tf_op jit(solution)/shard_map/all_to_all | solution.py:340
  57.5 28.4 %all-to-all-start.2 = ((bf16[128,8,128]{2,1,0:T(8,128)(2,1)}), bf16[128,8,128]{2,1,0:T(8,128)(2,1)S(1)}, u32[]{:S(2)}, u32[]{:S(2)}) async-start(bf16[128,8,128]{2,1,0:T(8,128)(2,1)} %pack_cols.1), calls=%async_computation.2 | async-start | bytes 524288 | tf_op jit(solution)/shard_map/all_to_all | solution.py:355
  67.0 5.8 %collective-permute-start.2 = (bf16[32,384]{1,0:T(8,128)(2,1)S(1)}, bf16[32,384]{1,0:T(8,128)(2,1)S(1)}, u32[]{:S(2)}, u32[]{:S(2)}) collective-permute-start(bf16[32,384]{1,0:T(8,128)(2,1)S(1)} %get-tuple-element.35), channel_id=1, source_target_pairs={{0,2},{1,3},{2,0},{3,1},{4,6},{5,7},{6,4},{7,5},{8,10},{9,11},{10,... | collective-permute-start | bytes 73736 | tf_op jit(solution)/shard_map/ppermute | solution.py:329

commit v2 on v1

--- a/solution.py
+++ b/solution.py
@@ -29,6 +29,11 @@
     i = lax.broadcasted_iota(jnp.int32, (L, L), 0)
     j = lax.broadcasted_iota(jnp.int32, (L, L), 1)
     return (i <= j).astype(dtype)
+
+
+def head_lanes():
+    lane = lax.broadcasted_iota(jnp.int32, (1, L), 1)
+    return (lane < HD).astype(BF16), (lane >= HD).astype(BF16)
 
 
 def split3(x):
@@ -61,7 +66,7 @@
         copy.start()
     for copy in copies[:4]:
         copy.wait()
-    keep = keep_of(tis_ref[...], n)
+    keep = keep_of(tis_ref[...], n).astype(BF16)
     for k in range(blocks):
         at = pl.ds(k * L, L)
         uv = jnp.concatenate([u_ref[:, at].astype(F32), v_ref[:, at].astype(F32)], axis=0)
@@ -74,8 +79,8 @@
             copies[4 + o + r].wait()
             for k in range(blocks):
                 at = pl.ds(k * L, L)
-                part = ref[pl.ds(r * L, L), at].astype(F32) * keep[:, k * L : (k + 1) * L]
-                scr[:, per * k + o + r, :] = part.T
+                part = ref[pl.ds(r * L, L), at] * keep[:, k * L : (k + 1) * L]
+                scr[:, per * k + o + r, :] = part.T.astype(F32)
     send_out(scr, send_ref, send_any, out_sems)
 
 
@@ -92,7 +97,7 @@
         copy.wait()
 
 
-def row_kernel(x_ref, w_ref, tis_ref, u_ref, v_ref, a_ref, dx_ref, d0_ref, d1_ref, d2_ref, d3_ref, da_ref, y_ref, duv_ref, xm_ref, wm_ref, wt_ref):
+def row_kernel(x_ref, w_ref, tis_ref, u_ref, v_ref, a_ref, dx_ref, own_ref, give_ref, da_ref, y_ref, duv_ref, xm_ref, wm_ref, wt_ref):
     n = x_ref.shape[1]
     keep = keep_of(tis_ref[...], n).astype(BF16)
     xm_ref[...] = x_ref[...] * keep
@@ -155,9 +160,12 @@
             duv_ref[pl.ds(2 * quarter * k, quarter), at] = du[b][quarter * k : quarter * (k + 1)]
             duv_ref[pl.ds(2 * quarter * k + quarter, quarter), at] = dv[b][quarter * k : quarter * (k + 1)]
     me = lax.axis_index("heads")
-    for shift, ref in enumerate((d0_ref, d1_ref, d2_ref, d3_ref)):
-        part = lax.rem(me + shift, 4) * (2 * quarter)
-        ref[...] = duv_ref[pl.ds(pl.multiple_of(part, 2 * quarter), 2 * quarter), :].astype(ref.dtype)
+    part = 2 * quarter
+    for slot, near in enumerate((me, lax.rem(me + 2, 4))):
+        far = near + 1 - 2 * lax.rem(near, 2)
+        to = pl.ds(slot * part, part)
+        own_ref[to, :] = duv_ref[pl.ds(pl.multiple_of(near * part, part), part), :]
+        give_ref[to, :] = duv_ref[pl.ds(pl.multiple_of(far * part, part), part), :].astype(give_ref.dtype)
     suffix = (i0 >= i1).astype(BF16)
     later = jnp.zeros((heads, 1), F32)
     for b in reversed(range(blocks)):
@@ -170,7 +178,7 @@
         da_ref[:, at] = da.astype(BF16)
 
 
-def col_pair_kernel(recv_ref, after0_ref, after1_ref, hop_any, a_ref, xt_ref, wt_ref, scr, d_ref, hop_ref, sems, *, blocks, heads):
+def col_pair_kernel(recv_ref, after_ref, hop_any, a_ref, xt_ref, wt_ref, scr, d_ref, hop_ref, sems, *, blocks, heads):
     scr[...] = recv_ref[...].astype(F32)
     halves = heads // 2
     per = 2 * halves + 1
@@ -178,6 +186,7 @@
     i0 = lax.broadcasted_iota(jnp.int32, (L, L), 0)
     i1 = lax.broadcasted_iota(jnp.int32, (L, L), 1)
     later = i0 <= i1
+    half = head_lanes()
     gcol = tn(tri, scr[:, per * blocks, :].astype(BF16))
     grow = gcol.T
     quarter = HD // 4
@@ -190,12 +199,12 @@
         u, v = uv[:HD], uv[HD:]
         q = None
         for h in range(heads):
-            ch = pl.ds(h * HD, HD)
             c = heads * k + h
             d = jnp.exp(jnp.minimum(grow[c : c + 1, :] - gcol[:, c : c + 1], 0.0))
             d = jnp.where(later, d, 0.0)
             d_ref[c] = d
-            dm = d * nt(xt_ref[k, :, ch], wt_ref[k, :, ch])
+            pair = pl.ds(h // 2 * L, L)
+            dm = d * nt(xt_ref[k, :, pair] * half[h % 2], wt_ref[k, :, pair])
             q = dm if q is None else q + dm
         qb = q.astype(BF16)
         du = nt(v, qb).astype(BF16)
@@ -215,21 +224,26 @@
         copy.wait()
 
 
-def col_value_kernel(a_ref, xt_ref, wt_ref, ret_ref, da_ref, y_ref, dx_ref, *, blocks, heads):
+def col_value_kernel(a_ref, xt_ref, wt_ref, own_ref, near_ref, ret_ref, da_ref, mine_ref, pass_ref, y_ref, dx_ref, *, blocks, heads):
+    part = mine_ref.shape[0]
+    mine_ref[...] = own_ref[:part] + near_ref[:part].astype(F32)
+    pass_ref[...] = (own_ref[part:] + near_ref[part:].astype(F32)).astype(pass_ref.dtype)
     i0 = lax.broadcasted_iota(jnp.int32, (L, L), 0)
     i1 = lax.broadcasted_iota(jnp.int32, (L, L), 1)
     suffix = (i0 >= i1).astype(BF16)
+    half = head_lanes()
     rows = da_ref.shape[0]
     width = heads * HD
     c0 = lax.broadcasted_iota(jnp.int32, (rows, width), 0)
     c1 = lax.broadcasted_iota(jnp.int32, (rows, width), 1)
     dg = jnp.zeros((rows, L), F32)
     for k in range(blocks):
-        for h in range(heads):
-            ch = pl.ds(h * HD, HD)
-            a = a_ref[heads * k + h]
-            dx_ref[:, ch] = nn(a, wt_ref[k, :, ch])
-            y_ref[:, ch] = tn(a, xt_ref[k, :, ch])
+        for r in range(heads // 2):
+            pair = pl.ds(r * L, L)
+            a0, a1 = a_ref[heads * k + 2 * r], a_ref[heads * k + 2 * r + 1]
+            w, x = wt_ref[k, :, pair], xt_ref[k, :, pair]
+            dx_ref[:, pair] = nn(jnp.concatenate([a0, a1], axis=1), jnp.concatenate([w * half[0], w * half[1]], axis=0))
+            y_ref[:, pair] = tn(jnp.concatenate([a0, a1], axis=0), jnp.concatenate([x * half[0], x * half[1]], axis=0))
         dx = dx_ref[...]
         for r in range(heads // 2):
             ret_ref[:, (heads // 2) * k + r, :] = dx[:, r * L : (r + 1) * L]
@@ -254,7 +268,7 @@
     send_out(scr, out_ref, out_any, sems)
 
 
-def final_kernel(back_ref, dx_ref, tis_ref, r0_ref, r1_ref, r2_ref, r3_ref, gx_ref, iu_ref, iv_ref, cu_ref, cv_ref, da_ref, scr, *, heads):
+def final_kernel(back_ref, dx_ref, tis_ref, mine_ref, other_ref, gx_ref, iu_ref, iv_ref, cu_ref, cv_ref, da_ref, scr, *, heads):
     n = dx_ref.shape[1]
     blocks = n // L
     halves = heads // 2
@@ -275,7 +289,7 @@
         cv_ref[:, at] = small[o + quarter : o + 2 * quarter].astype(BF16)
         o = 2 * quarter * blocks + heads * k
         da_ref[:, at] = small[o : o + heads].astype(BF16)
-    row = r0_ref[...] + r1_ref[...].astype(F32) + r2_ref[...].astype(F32) + r3_ref[...].astype(F32)
+    row = mine_ref[...] + other_ref[...].astype(F32)
     iu_ref[...] = row[:quarter].astype(BF16)
     iv_ref[...] = row[quarter:].astype(BF16)
 
@@ -319,15 +333,14 @@
     )(x, w, flat(inject_col), flat(readout_col), flat(decay_col), tissue)
     recv = lax.all_to_all(send, "rows", split_axis=0, concat_axis=0, tiled=True)
     share = (2 * quarter, n)
-    dx_row, mine, *theirs, da_row = call(
+    two = (4 * quarter, n)
+    dx_row, own, give, da_row = call(
         row_kernel,
-        [((chan, n), F32), (share, F32), (share, BF16), (share, BF16), (share, BF16), ((heads, n), BF16)],
+        [((chan, n), F32), (two, F32), (two, BF16), ((heads, n), BF16)],
         [vm((chan, n), F32), vm((2 * nstate, n), F32), vm((chan, n), BF16), vm((chan, n), BF16), vm((n, chan), BF16)],
         4 * 10**9, "row_scan",
     )(x, w, tissue, flat(inject_row), flat(readout_row), flat(decay_row))
-    shares = [
-        lax.ppermute(part, "heads", [(i, (i + shift) % 4) for i in range(4)]) for shift, part in enumerate(theirs, 1)
-    ]
+    near = lax.ppermute(give, "heads", [(i, i ^ 1) for i in range(4)])
     sizes = dict(blocks=blocks, heads=heads)
     hop_shape = (4, 2 * quarter * blocks, L)
     per_col = (blocks, L, chan)
@@ -336,16 +349,17 @@
         [(hop_shape, BF16, "far"), ((blocks * heads, L, L), BF16), (per_col, BF16), (per_col, BF16)],
         [vm(tile, F32), vm((blocks * heads, L, L), F32), vm(hop_shape, BF16), dma((blocks,))],
         10**9, "col_pairs",
-    )(recv, shares[0], shares[2])
+    )(recv, near)
     hopped = lax.all_to_all(hop, "heads", split_axis=0, concat_axis=0, tiled=True)
     used = blocks * heads // 2
     back_tile = (L, used + 2, L)
-    ret, da_col = call(
+    ret, da_col, mine, give = call(
         partial(col_value_kernel, **sizes),
-        [(back_tile, F32), ((16, L), F32)],
+        [(back_tile, F32), ((16, L), F32), (share, F32), (share, BF16)],
         [vm((L, chan), F32), vm((L, chan), F32)],
         2 * 10**9, "col_values",
-    )(weights, xt, wtc)
+    )(weights, xt, wtc, own, near)
+    other = lax.ppermute(give, "heads", [(i, i ^ 2) for i in range(4)])
     (packed,) = call(
         partial(pack_kernel, used=used),
         [(back_tile, BF16, "far")],
@@ -358,7 +372,7 @@
         [((chan, n), BF16)] + [((quarter, n), BF16)] * 4 + [((heads, n), BF16)],
         [vm(back_tile, F32)],
         10**7, "join",
-    )(back, dx_row, tissue, mine, *shares)
+    )(back, dx_row, tissue, mine, other)
     wide = lambda x: x.reshape(x.shape[0], 1, n)
     return wide(gx), wide(iu), wide(iv), wide(cu), wide(cv), wide(da_row), wide(da)
 

time: 87.4 us -> 85.5 us (0.978)
  starting transfers between devices: 39.5 us -> 35.8 us
  waiting for transfers between devices: 34.1 us -> 36.5 us
    ppermute x3 -> x2, waiting for transfers between devices: 6.16 us -> 8.3 us  [the longest x1 4.87 us: body(): near = lax.ppermute(give, 'heads', [(i, i ^ 1) for i in range(4)])]
    ppermute x3 -> x2, starting transfers between devices: 7.43 us -> 5.29 us  [the longest x1 2.96 us: body(): near = lax.ppermute(give, 'heads', [(i, i ^ 1) for i in range(4)])]
    all_to_all x1, starting transfers between devices: 9.49 us -> 7.87 us  [body(): lax.all_to_all(packed, 'rows', split_axis=0, concat_axis=0, tiled=True)]
  transfers between devices with their start and end apart: 6 -> 5, of which waited for: 5 -> 5; matrix products, arithmetic and copies ran while one was open for 0% -> 0% of each run, Pallas kernels for 5% -> 5%
where the time goes in v2:
time: 85.5 us; the launch traced here: 85.1 us
  waiting for transfers between devices  36.5 us (43%)
  starting transfers between devices  35.8 us (42%)
  Pallas kernels  11.4 us (13%)
    all_to_all x1, starting transfers between devices, body(): recv = lax.all_to_all(send, 'rows', split_axis=0, concat_axis=0, tiled=True)  19.3 us
    all_to_all x1, waiting for transfers between devices, body(): lax.all_to_all(packed, 'rows', split_axis=0, concat_axis=0, tiled=True)  13.2 us
    all_to_all x1, waiting for transfers between devices, body(): recv = lax.all_to_all(send, 'rows', split_axis=0, concat_axis=0, tiled=True)  12.6 us
    all_to_all x1, starting transfers between devices, body(): lax.all_to_all(packed, 'rows', split_axis=0, concat_axis=0, tiled=True)  7.87 us
    ppermute x1, waiting for transfers between devices, body(): near = lax.ppermute(give, 'heads', [(i, i ^ 1) for i in range(4)])  4.87 us
    ppermute x1, waiting for transfers between devices, body(): other = lax.ppermute(give, 'heads', [(i, i ^ 2) for i in range(4)])  3.43 us
    all_to_all x1, starting transfers between devices, body(): lax.all_to_all(hop, 'heads', split_axis=0, concat_axis=0, tiled=True)  3.31 us
    pallas_call x1, Pallas kernels, body(): call(row_kernel, [((chan, n), F32), (two, F32), (two, BF16), ((heads, n),...  3.27 us
  transfers between devices with their start and end apart: 5, of which 5 were waited for; matrix products, arithmetic and copies ran while one was open for 0% of the time, Pallas kernels for 5%

profile of v2, /device:TPU:9, one launch (start us, length us, event | category | flops | bytes accessed | tf_op | source)
XLA Modules:
  0.0 85.1 jit_solution(2985368077796894456)
XLA Ops:
  0.6 2.6 %pack_rows.1 = bf16[128,16,128]{2,1,0:T(8,128)(2,1)} custom-call(bf16[256,384]{1,0:T(8,128)(2,1)} %bitcast.15, bf16[256,384]{1,0:T(8,128)(2,1)} %bitcast.17, bf16[64,384]{1,0:T(8,128)(2,1)} %bitcast.22, bf16[64,384]{1,0:T(8,128)(2,1)} %bitcast.23, bf16[4,384]{1,0:T(4,128)(2,1)} %bitcast.24, s32[1,24]{1,0:T(1,128)} %tis_ref.3), custom_call_target="tpu_custom_call" | custom-call | flops 10000000 | bytes 1000000 | tf_op jit(solution)/shard_map/pack_rows/pallas_call | solution.py:324
  3.3 0.0 copy-start
  3.3 0.0 copy-start.1
  3.3 0.0 copy-start.3
  3.3 0.0 copy-start.4
  3.3 19.3 %all-to-all-start = ((bf16[128,16,128]{2,1,0:T(8,128)(2,1)}), bf16[128,16,128]{2,1,0:T(8,128)(2,1)S(1)}, u32[]{:S(2)}, u32[]{:S(2)}) async-start(bf16[128,16,128]{2,1,0:T(8,128)(2,1)} %pack_rows.1), calls=%async_computation | async-start | bytes 1048576 | tf_op jit(solution)/shard_map/all_to_all | solution.py:334
  22.6 0.0 copy-start.5
  22.6 0.0 copy-start.2
  22.6 0.0 copy-done
  22.6 0.0 copy-done.1
  22.7 0.0 copy-done.3
  22.7 0.0 copy-done.4
  22.7 0.6 copy-done.5
  23.3 0.0 copy-done.2
  23.3 3.3 %row_scan.1 = (f32[256,384]{1,0:T(8,128)S(1)}, f32[64,384]{1,0:T(8,128)S(1)}, bf16[64,384]{1,0:T(8,128)(2,1)S(1)}, bf16[4,384]{1,0:T(4,128)(2,1)}) custom-call(bf16[256,384]{1,0:T(8,128)(2,1)S(1)} %bitcast.16, bf16[256,384]{1,0:T(8,128)(2,1)S(1)} %bitcast.18, s32[1,24]{1,0:T(1,128)S(1)} %copy-done.2, bf16[64,384]{1,0:T(8,128)(2,1)S(1)} %bitcast.19, ...), custom_call_target="tpu_custom_call" | custom-call | flops 4000000000 | bytes 1000000 | tf_op jit(solution)/shard_map/row_scan/pallas_call | solution.py:337
  26.6 3.0 %collective-permute-start = (bf16[64,384]{1,0:T(8,128)(2,1)S(1)}, bf16[64,384]{1,0:T(8,128)(2,1)S(1)}, u32[]{:S(2)}, u32[]{:S(2)}) collective-permute-start(bf16[64,384]{1,0:T(8,128)(2,1)S(1)} %get-tuple-element.25), channel_id=1, source_target_pairs={{0,1},{1,0},{2,3},{3,2},{4,5},{5,4},{6,7},{7,6},{8,9},{9,8},{10,11... | collective-permute-start | bytes 147464 | tf_op jit(solution)/shard_map/ppermute | solution.py:343
  29.5 4.9 %collective-permute-done.after_ref.near_ref = bf16[64,384]{1,0:T(8,128)(2,1)S(1)} collective-permute-done((bf16[64,384]{1,0:T(8,128)(2,1)S(1)}, bf16[64,384]{1,0:T(8,128)(2,1)S(1)}, u32[]{:S(2)}, u32[]{:S(2)}) %collective-permute-start) | collective-permute-done | bytes 49184 | tf_op jit(solution)/shard_map/ppermute | solution.py:343
  34.4 12.6 %all-to-all-done.recv_ref = bf16[128,16,128]{2,1,0:T(8,128)(2,1)S(1)} async-done(((bf16[128,16,128]{2,1,0:T(8,128)(2,1)}), bf16[128,16,128]{2,1,0:T(8,128)(2,1)S(1)}, u32[]{:S(2)}, u32[]{:S(2)}) %all-to-all-start) | async-done | bytes 524320 | tf_op jit(solution)/shard_map/all_to_all | solution.py:334
  47.0 2.5 %col_pairs.1 = (bf16[4,96,128]{2,1,0:T(8,128)(2,1)}, bf16[12,128,128]{2,1,0:T(8,128)(2,1)S(1)}, bf16[3,128,256]{2,1,0:T(8,128)(2,1)S(1)}, bf16[3,128,256]{2,1,0:T(8,128)(2,1)S(1)}) custom-call(bf16[128,16,128]{2,1,0:T(8,128)(2,1)S(1)} %all-to-all-done.recv_ref, bf16[64,384]{1,0:T(8,128)(2,1)S(1)} %collective-permute-done.after_ref.near_ref), custom_call_target="tpu_custom_call" | custom-call | flops 1000000000 | bytes 1000000 | tf_op jit(solution)/shard_map/col_pairs/pallas_call | solution.py:347
  49.5 3.3 %all-to-all-start.1 = ((bf16[4,96,128]{2,1,0:T(8,128)(2,1)}), bf16[4,96,128]{2,1,0:T(8,128)(2,1)S(1)}, u32[]{:S(2)}, u32[]{:S(2)}) async-start(bf16[4,96,128]{2,1,0:T(8,128)(2,1)} %get-tuple-element.26), calls=%async_computation.1 | async-start | bytes 196608 | tf_op jit(solution)/shard_map/all_to_all | solution.py:353
  52.8 1.1 %col_values.1 = (f32[128,8,128]{2,1,0:T(8,128)S(1)}, f32[16,128]{1,0:T(8,128)S(1)}, f32[32,384]{1,0:T(8,128)S(1)}, bf16[32,384]{1,0:T(8,128)(2,1)S(1)}) custom-call(bf16[12,128,128]{2,1,0:T(8,128)(2,1)S(1)} %get-tuple-element.27.a_ref, bf16[3,128,256]{2,1,0:T(8,128)(2,1)S(1)} %get-tuple-element.28.xt_ref, bf16[3,128,256]{2,1,0:T(8,128)(2,1)S(1)} %get-tuple-element.29.wt_ref, ...), custom_call_target="tpu_custom_call" | custom-call | flops 2000000000 | bytes 1000000 | tf_op jit(solution)/shard_map/col_values/pallas_call | solution.py:356
  53.9 2.4 %all-to-all-done.1.hop_ref = bf16[4,96,128]{2,1,0:T(8,128)(2,1)S(1)} async-done(((bf16[4,96,128]{2,1,0:T(8,128)(2,1)}), bf16[4,96,128]{2,1,0:T(8,128)(2,1)S(1)}, u32[]{:S(2)}, u32[]{:S(2)}) %all-to-all-start.1) | async-done | bytes 98336 | tf_op jit(solution)/shard_map/all_to_all | solution.py:353
  56.3 0.8 pack_cols.1
  57.1 7.9 %all-to-all-start.2 = ((bf16[128,8,128]{2,1,0:T(8,128)(2,1)}), bf16[128,8,128]{2,1,0:T(8,128)(2,1)S(1)}, u32[]{:S(2)}, u32[]{:S(2)}) async-start(bf16[128,8,128]{2,1,0:T(8,128)(2,1)} %pack_cols.1), calls=%async_computation.2 | async-start | bytes 524288 | tf_op jit(solution)/shard_map/all_to_all | solution.py:369
  65.0 2.3 %collective-permute-start.1 = (bf16[32,384]{1,0:T(8,128)(2,1)S(1)}, bf16[32,384]{1,0:T(8,128)(2,1)S(1)}, u32[]{:S(2)}, u32[]{:S(2)}) collective-permute-start(bf16[32,384]{1,0:T(8,128)(2,1)S(1)} %get-tuple-element.35), channel_id=1, source_target_pairs={{0,2},{1,3},{2,0},{3,1},{4,6},{5,7},{6,4},{7,5},{8,10},{9,11},{10,... | collective-permute-start | bytes 73736 | tf_op jit(solution)/shard_map/ppermute | solution.py:362
  67.3 3.4 %collective-permute-done.1.other_ref = bf16[32,384]{1,0:T(8,128)(2,1)S(1)} collective-permute-done((bf16[32,384]{1,0:T(8,128)(2,1)S(1)}, bf16[32,384]{1,0:T(8,128)(2,1)S(1)}, u32[]{:S(2)}, u32[]{:S(2)}) %collective-permute-start.1) | collective-permute-done | bytes 24608 | tf_op jit(solution)/shard_map/ppermute | solution.py:362
  70.8 13.2 %all-to-all-done.2.back_ref = bf16[128,8,128]{2,1,0:T(8,128)(2,1)S(1)} async-done(((bf16[128,8,128]{2,1,0:T(8,128)(2,1)}), bf16[128,8,128]{2,1,0:T(8,128)(2,1)S(1)}, u32[]{:S(2)}, u32[]{:S(2)}) %all-to-all-start.2) | async-done | bytes 262176 | tf_op jit(solution)/shard_map/all_to_all | solution.py:369
  84.0 1.0 %join.1 = (bf16[256,384]{1,0:T(8,128)(2,1)}, bf16[16,384]{1,0:T(8,128)(2,1)}, bf16[16,384]{1,0:T(8,128)(2,1)}, bf16[16,384]{1,0:T(8,128)(2,1)}, bf16[16,384]{1,0:T(8,128)(2,1)}, /*index=5*/bf16[4,384]{1,0:T(4,128)(2,1)}) custom-call(bf16[128,8,128]{2,1,0:T(8,128)(2,1)S(1)} %all-to-all-done.2.back_ref, f32[256,384]{1,0:T(8,128)S(1)} %get-tuple-element.33.dx_ref, ...), custom_call_target="tpu_custom_call" | custom-call | flops 10000000 | bytes 1000000 | tf_op jit(solution)/shard_map/join/pallas_call | solution.py:370
Async XLA Ops:
  3.3 19.4 %copy-start = (bf16[256,1,384]{2,0,1:T(8,128)(2,1)S(1)}, bf16[256,1,384]{2,0,1:T(8,128)(2,1)}, u32[]{:S(2)}) copy-start(bf16[256,1,384]{2,0,1:T(8,128)(2,1)} %param.9) | copy-start | bytes 589828
  3.3 19.4 %copy-start.1 = (bf16[256,1,384]{2,0,1:T(8,128)(2,1)S(1)}, bf16[256,1,384]{2,0,1:T(8,128)(2,1)}, u32[]{:S(2)}) copy-start(bf16[256,1,384]{2,0,1:T(8,128)(2,1)} %param.10) | copy-start | bytes 589828
  3.3 19.4 %copy-start.3 = (bf16[64,1,384]{2,0,1:T(8,128)(2,1)S(1)}, bf16[64,1,384]{2,0,1:T(8,128)(2,1)}, u32[]{:S(2)}) copy-start(bf16[64,1,384]{2,0,1:T(8,128)(2,1)} %param.11) | copy-start | bytes 147460
  3.3 19.4 %copy-start.4 = (bf16[64,1,384]{2,0,1:T(8,128)(2,1)S(1)}, bf16[64,1,384]{2,0,1:T(8,128)(2,1)}, u32[]{:S(2)}) copy-start(bf16[64,1,384]{2,0,1:T(8,128)(2,1)} %param.12) | copy-start | bytes 147460
  3.3 43.7 %all-to-all-start = ((bf16[128,16,128]{2,1,0:T(8,128)(2,1)}), bf16[128,16,128]{2,1,0:T(8,128)(2,1)S(1)}, u32[]{:S(2)}, u32[]{:S(2)}) async-start(bf16[128,16,128]{2,1,0:T(8,128)(2,1)} %pack_rows.1), calls=%async_computation | async-start | bytes 1048576 | tf_op jit(solution)/shard_map/all_to_all | solution.py:334
  22.6 0.7 copy-start.5
  22.6 0.7 copy-start.2
  26.6 7.8 %collective-permute-start = (bf16[64,384]{1,0:T(8,128)(2,1)S(1)}, bf16[64,384]{1,0:T(8,128)(2,1)S(1)}, u32[]{:S(2)}, u32[]{:S(2)}) collective-permute-start(bf16[64,384]{1,0:T(8,128)(2,1)S(1)} %get-tuple-element.25), channel_id=1, source_target_pairs={{0,1},{1,0},{2,3},{3,2},{4,5},{5,4},{6,7},{7,6},{8,9},{9,8},{10,11... | collective-permute-start | bytes 147464 | tf_op jit(solution)/shard_map/ppermute | solution.py:343
  49.5 6.8 %all-to-all-start.1 = ((bf16[4,96,128]{2,1,0:T(8,128)(2,1)}), bf16[4,96,128]{2,1,0:T(8,128)(2,1)S(1)}, u32[]{:S(2)}, u32[]{:S(2)}) async-start(bf16[4,96,128]{2,1,0:T(8,128)(2,1)} %get-tuple-element.26), calls=%async_computation.1 | async-start | bytes 196608 | tf_op jit(solution)/shard_map/all_to_all | solution.py:353
  57.1 26.9 %all-to-all-start.2 = ((bf16[128,8,128]{2,1,0:T(8,128)(2,1)}), bf16[128,8,128]{2,1,0:T(8,128)(2,1)S(1)}, u32[]{:S(2)}, u32[]{:S(2)}) async-start(bf16[128,8,128]{2,1,0:T(8,128)(2,1)} %pack_cols.1), calls=%async_computation.2 | async-start | bytes 524288 | tf_op jit(solution)/shard_map/all_to_all | solution.py:369
  65.0 5.8 %collective-permute-start.1 = (bf16[32,384]{1,0:T(8,128)(2,1)S(1)}, bf16[32,384]{1,0:T(8,128)(2,1)S(1)}, u32[]{:S(2)}, u32[]{:S(2)}) collective-permute-start(bf16[32,384]{1,0:T(8,128)(2,1)S(1)} %get-tuple-element.35), channel_id=1, source_target_pairs={{0,2},{1,3},{2,0},{3,1},{4,6},{5,7},{6,4},{7,5},{8,10},{9,11},{10,... | collective-permute-start | bytes 73736 | tf_op jit(solution)/shard_map/ppermute | solution.py:362

commit v3 on v2

--- a/solution.py
+++ b/solution.py
@@ -178,80 +178,63 @@
         da_ref[:, at] = da.astype(BF16)
 
 
-def col_pair_kernel(recv_ref, after_ref, hop_any, a_ref, xt_ref, wt_ref, scr, d_ref, hop_ref, sems, *, blocks, heads):
+def col_kernel(recv_ref, own_ref, near_ref, hop_ref, ret_ref, da_ref, mine_ref, pass_ref, scr, y_ref, dx_ref, *, blocks, heads):
+    part = mine_ref.shape[0]
+    mine_ref[...] = own_ref[:part] + near_ref[:part].astype(F32)
+    pass_ref[...] = (own_ref[part:] + near_ref[part:].astype(F32)).astype(pass_ref.dtype)
     scr[...] = recv_ref[...].astype(F32)
     halves = heads // 2
     per = 2 * halves + 1
-    tri = upper(BF16)
+    half = head_lanes()
     i0 = lax.broadcasted_iota(jnp.int32, (L, L), 0)
     i1 = lax.broadcasted_iota(jnp.int32, (L, L), 1)
     later = i0 <= i1
-    half = head_lanes()
-    gcol = tn(tri, scr[:, per * blocks, :].astype(BF16))
+    gcol = nn((i1 <= i0).astype(BF16), scr[:, per * blocks, :].astype(BF16))
     grow = gcol.T
     quarter = HD // 4
-    copies = []
-    for k in range(blocks):
-        for r in range(halves):
-            xt_ref[k, :, pl.ds(r * L, L)] = scr[:, per * k + r, :].astype(BF16)
-            wt_ref[k, :, pl.ds(r * L, L)] = scr[:, per * k + halves + r, :].astype(BF16)
-        uv = scr[:, per * k + 2 * halves, :].T.astype(BF16)
-        u, v = uv[:HD], uv[HD:]
-        q = None
-        for h in range(heads):
-            c = heads * k + h
-            d = jnp.exp(jnp.minimum(grow[c : c + 1, :] - gcol[:, c : c + 1], 0.0))
-            d = jnp.where(later, d, 0.0)
-            d_ref[c] = d
-            pair = pl.ds(h // 2 * L, L)
-            dm = d * nt(xt_ref[k, :, pair] * half[h % 2], wt_ref[k, :, pair])
-            q = dm if q is None else q + dm
-        qb = q.astype(BF16)
-        du = nt(v, qb).astype(BF16)
-        dv = nn(u, qb).astype(BF16)
-        at = pl.ds(2 * quarter * k, 2 * quarter)
-        for p in range(4):
-            hop_ref[p, pl.ds(2 * quarter * k, quarter), :] = du[quarter * p : quarter * (p + 1)]
-            hop_ref[p, pl.ds(2 * quarter * k + quarter, quarter), :] = dv[quarter * p : quarter * (p + 1)]
-        copies.append(pltpu.make_async_copy(hop_ref.at[:, at], hop_any.at[:, at], sems.at[k]))
-        copies[-1].start()
-    for k in range(blocks):
-        uvt = scr[:, per * k + 2 * halves, :]
-        s = nn(uvt[:, :HD].astype(BF16), uvt.T[HD:].astype(BF16))
-        for h in range(heads):
-            a_ref[heads * k + h] = (d_ref[heads * k + h] * s).astype(BF16)
-    for copy in copies:
-        copy.wait()
-
-
-def col_value_kernel(a_ref, xt_ref, wt_ref, own_ref, near_ref, ret_ref, da_ref, mine_ref, pass_ref, y_ref, dx_ref, *, blocks, heads):
-    part = mine_ref.shape[0]
-    mine_ref[...] = own_ref[:part] + near_ref[:part].astype(F32)
-    pass_ref[...] = (own_ref[part:] + near_ref[part:].astype(F32)).astype(pass_ref.dtype)
-    i0 = lax.broadcasted_iota(jnp.int32, (L, L), 0)
-    i1 = lax.broadcasted_iota(jnp.int32, (L, L), 1)
-    suffix = (i0 >= i1).astype(BF16)
-    half = head_lanes()
     rows = da_ref.shape[0]
     width = heads * HD
     c0 = lax.broadcasted_iota(jnp.int32, (rows, width), 0)
     c1 = lax.broadcasted_iota(jnp.int32, (rows, width), 1)
     dg = jnp.zeros((rows, L), F32)
     for k in range(blocks):
-        for r in range(heads // 2):
+        uvt = scr[:, per * k + 2 * halves, :]
+        uv = uvt.T.astype(BF16)
+        u, v = uv[:HD], uv[HD:]
+        s = nn(uvt[:, :HD].astype(BF16), v)
+        q = None
+        xs = [scr[:, per * k + r, :] for r in range(halves)]
+        ws = [scr[:, per * k + halves + r, :] for r in range(halves)]
+        for r in range(halves):
             pair = pl.ds(r * L, L)
-            a0, a1 = a_ref[heads * k + 2 * r], a_ref[heads * k + 2 * r + 1]
-            w, x = wt_ref[k, :, pair], xt_ref[k, :, pair]
-            dx_ref[:, pair] = nn(jnp.concatenate([a0, a1], axis=1), jnp.concatenate([w * half[0], w * half[1]], axis=0))
-            y_ref[:, pair] = tn(jnp.concatenate([a0, a1], axis=0), jnp.concatenate([x * half[0], x * half[1]], axis=0))
+            x, w = xs[r].astype(BF16), ws[r].astype(BF16)
+            x_of = [x * half[0], x * half[1]]
+            w_of = [w * half[0], w * half[1]]
+            a = []
+            for h in range(2):
+                c = heads * k + 2 * r + h
+                d = jnp.exp(jnp.minimum(grow[c : c + 1, :] - gcol[:, c : c + 1], 0.0))
+                d = jnp.where(later, d, 0.0)
+                dm = d * nt(x_of[h], w)
+                q = dm if q is None else q + dm
+                a.append((d * s).astype(BF16))
+            dx_ref[:, pair] = nn(jnp.concatenate(a, axis=1), jnp.concatenate(w_of, axis=0))
+            y_ref[:, pair] = tn(jnp.concatenate(a, axis=0), jnp.concatenate(x_of, axis=0))
+        qb = q.astype(BF16)
+        du = nt(v, qb).astype(BF16)
+        dv = nn(u, qb).astype(BF16)
+        for p in range(4):
+            hop_ref[p, pl.ds(2 * quarter * k, quarter), :] = du[quarter * p : quarter * (p + 1)]
+            hop_ref[p, pl.ds(2 * quarter * k + quarter, quarter), :] = dv[quarter * p : quarter * (p + 1)]
         dx = dx_ref[...]
-        for r in range(heads // 2):
-            ret_ref[:, (heads // 2) * k + r, :] = dx[:, r * L : (r + 1) * L]
-        e = wt_ref[k].astype(F32) * y_ref[...] - xt_ref[k].astype(F32) * dx
+        for r in range(halves):
+            ret_ref[:, halves * k + r, :] = dx[:, r * L : (r + 1) * L]
+        e = jnp.concatenate(ws, axis=1) * y_ref[...] - jnp.concatenate(xs, axis=1) * dx
         start = (c0 - heads * k) * HD
         seg = ((c1 >= start) & (c1 < start + HD)).astype(BF16)
-        for part in split3(e):
-            dg += nt(seg, part)
+        for term in split3(e):
+            dg += nt(seg, term)
+    suffix = (i0 >= i1).astype(BF16)
     hi, mid, lo = split3(dg)
     da_ref[...] = nn(hi, suffix) + nn(mid, suffix) + nn(lo, suffix)
 
@@ -327,7 +310,7 @@
         [
             vm((chan, n), BF16), vm((chan, n), BF16), vm((nstate, n), BF16), vm((nstate, n), BF16),
             vm((heads, n), BF16), vm(tissue.shape, jnp.int32), vm(tile, BF16), vm(tile, F32),
-            dma((4 + 2 * chan // L,)), dma((8,)),
+            dma((4 + 2 * chan // L,)), dma((4,)),
         ],
         10**7, "pack_rows", 60, [True] * 6,
     )(x, w, flat(inject_col), flat(readout_col), flat(decay_col), tissue)
@@ -341,24 +324,15 @@
         4 * 10**9, "row_scan",
     )(x, w, tissue, flat(inject_row), flat(readout_row), flat(decay_row))
     near = lax.ppermute(give, "heads", [(i, i ^ 1) for i in range(4)])
-    sizes = dict(blocks=blocks, heads=heads)
-    hop_shape = (4, 2 * quarter * blocks, L)
-    per_col = (blocks, L, chan)
-    hop, weights, xt, wtc = call(
-        partial(col_pair_kernel, **sizes),
-        [(hop_shape, BF16, "far"), ((blocks * heads, L, L), BF16), (per_col, BF16), (per_col, BF16)],
-        [vm(tile, F32), vm((blocks * heads, L, L), F32), vm(hop_shape, BF16), dma((blocks,))],
-        10**9, "col_pairs",
-    )(recv, near)
-    hopped = lax.all_to_all(hop, "heads", split_axis=0, concat_axis=0, tiled=True)
     used = blocks * heads // 2
     back_tile = (L, used + 2, L)
-    ret, da_col, mine, give = call(
-        partial(col_value_kernel, **sizes),
-        [(back_tile, F32), ((16, L), F32), (share, F32), (share, BF16)],
-        [vm((L, chan), F32), vm((L, chan), F32)],
-        2 * 10**9, "col_values",
-    )(weights, xt, wtc, own, near)
+    hop, ret, da_col, mine, give = call(
+        partial(col_kernel, blocks=blocks, heads=heads),
+        [((4, 2 * quarter * blocks, L), BF16), (back_tile, F32), ((16, L), F32), (share, F32), (share, BF16)],
+        [vm(tile, F32), vm((L, chan), F32), vm((L, chan), F32)],
+        10**9, "col_scan",
+    )(recv, own, near)
+    hopped = lax.all_to_all(hop, "heads", split_axis=0, concat_axis=0, tiled=True)
     other = lax.ppermute(give, "heads", [(i, i ^ 2) for i in range(4)])
     (packed,) = call(
         partial(pack_kernel, used=used),

time: 85.5 us -> 84.9 us (level)
  blocking collectives: 0 us -> 6.57 us
  starting transfers between devices: 35.8 us -> 31.9 us
  waiting for transfers between devices: 36.5 us -> 34.2 us
    all_to_all x0 -> x1, blocking collectives: none -> 6.57 us  [body(): lax.all_to_all(hop, 'heads', split_axis=0, concat_axis=0, tiled=True)]
    all_to_all x1 -> x0, starting transfers between devices: 3.31 us -> none  [body(): lax.all_to_all(hop, 'heads', split_axis=0, concat_axis=0, tiled=True)]
    all_to_all x1 -> x0, waiting for transfers between devices: 2.37 us -> none  [body(): lax.all_to_all(hop, 'heads', split_axis=0, concat_axis=0, tiled=True)]
    pallas_call x2 -> x1, Pallas kernels: 3.63 us -> 2.8 us  [body(): call(partial(col_kernel, blocks=blocks, heads=heads), [((4, 2 * quarter *...]
  transfers between devices with their start and end apart: 5 -> 4, of which waited for: 5 -> 4; matrix products, arithmetic and copies ran while one was open for 0% -> 0% of each run, Pallas kernels for 5% -> 4%
where the time goes in v3:
time: 84.9 us; the launch traced here: 84.6 us
  waiting for transfers between devices  34.2 us (40%)
  starting transfers between devices  31.9 us (38%)
  Pallas kernels  10.6 us (12%)
  blocking collectives  6.57 us (8%)
    all_to_all x1, starting transfers between devices, body(): recv = lax.all_to_all(send, 'rows', split_axis=0, concat_axis=0, tiled=True)  19.3 us
    all_to_all x1, waiting for transfers between devices, body(): lax.all_to_all(packed, 'rows', split_axis=0, concat_axis=0, tiled=True)  13.1 us
    all_to_all x1, waiting for transfers between devices, body(): recv = lax.all_to_all(send, 'rows', split_axis=0, concat_axis=0, tiled=True)  12.6 us
    all_to_all x1, starting transfers between devices, body(): lax.all_to_all(packed, 'rows', split_axis=0, concat_axis=0, tiled=True)  7.43 us
    all_to_all x1, blocking collectives, body(): lax.all_to_all(hop, 'heads', split_axis=0, concat_axis=0, tiled=True)  6.57 us
    ppermute x1, waiting for transfers between devices, body(): near = lax.ppermute(give, 'heads', [(i, i ^ 1) for i in range(4)])  4.87 us
    ppermute x1, waiting for transfers between devices, body(): other = lax.ppermute(give, 'heads', [(i, i ^ 2) for i in range(4)])  3.6 us
    pallas_call x1, Pallas kernels, body(): call(row_kernel, [((chan, n), F32), (two, F32), (two, BF16), ((heads, n),...  3.27 us
  transfers between devices with their start and end apart: 4, of which 4 were waited for; matrix products, arithmetic and copies ran while one was open for 0% of the time, Pallas kernels for 4%

profile of v3, /device:TPU:9, one launch (start us, length us, event | category | flops | bytes accessed | tf_op | source)
XLA Modules:
  0.0 84.6 jit_solution(16197286777422773440)
XLA Ops:
  0.6 2.6 %pack_rows.1 = bf16[128,16,128]{2,1,0:T(8,128)(2,1)} custom-call(bf16[256,384]{1,0:T(8,128)(2,1)} %bitcast.15, bf16[256,384]{1,0:T(8,128)(2,1)} %bitcast.17, bf16[64,384]{1,0:T(8,128)(2,1)} %bitcast.22, bf16[64,384]{1,0:T(8,128)(2,1)} %bitcast.23, bf16[4,384]{1,0:T(4,128)(2,1)} %bitcast.24, s32[1,24]{1,0:T(1,128)} %tis_ref.3), custom_call_target="tpu_custom_call" | custom-call | flops 10000000 | bytes 1000000 | tf_op jit(solution)/shard_map/pack_rows/pallas_call | solution.py:307
  3.2 0.0 copy-start
  3.3 0.0 copy-start.1
  3.3 0.0 copy-start.3
  3.3 0.0 copy-start.4
  3.3 19.3 %all-to-all-start = ((bf16[128,16,128]{2,1,0:T(8,128)(2,1)}), bf16[128,16,128]{2,1,0:T(8,128)(2,1)S(1)}, u32[]{:S(2)}, u32[]{:S(2)}) async-start(bf16[128,16,128]{2,1,0:T(8,128)(2,1)} %pack_rows.1), calls=%async_computation | async-start | bytes 1048576 | tf_op jit(solution)/shard_map/all_to_all | solution.py:317
  22.6 0.0 copy-start.5
  22.6 0.0 copy-start.2
  22.6 0.0 copy-done
  22.6 0.0 copy-done.1
  22.6 0.0 copy-done.3
  22.6 0.0 copy-done.4
  22.7 0.6 copy-done.5
  23.3 0.0 copy-done.2
  23.3 3.3 %row_scan.1 = (f32[256,384]{1,0:T(8,128)S(1)}, f32[64,384]{1,0:T(8,128)S(1)}, bf16[64,384]{1,0:T(8,128)(2,1)S(1)}, bf16[4,384]{1,0:T(4,128)(2,1)}) custom-call(bf16[256,384]{1,0:T(8,128)(2,1)S(1)} %bitcast.16, bf16[256,384]{1,0:T(8,128)(2,1)S(1)} %bitcast.18, s32[1,24]{1,0:T(1,128)S(1)} %copy-done.2, bf16[64,384]{1,0:T(8,128)(2,1)S(1)} %bitcast.19, ...), custom_call_target="tpu_custom_call" | custom-call | flops 4000000000 | bytes 1000000 | tf_op jit(solution)/shard_map/row_scan/pallas_call | solution.py:320
  26.6 3.0 %collective-permute-start = (bf16[64,384]{1,0:T(8,128)(2,1)S(1)}, bf16[64,384]{1,0:T(8,128)(2,1)S(1)}, u32[]{:S(2)}, u32[]{:S(2)}) collective-permute-start(bf16[64,384]{1,0:T(8,128)(2,1)S(1)} %get-tuple-element.23), channel_id=1, source_target_pairs={{0,1},{1,0},{2,3},{3,2},{4,5},{5,4},{6,7},{7,6},{8,9},{9,8},{10,11... | collective-permute-start | bytes 147464 | tf_op jit(solution)/shard_map/ppermute | solution.py:326
  29.5 4.9 %collective-permute-done.near_ref = bf16[64,384]{1,0:T(8,128)(2,1)S(1)} collective-permute-done((bf16[64,384]{1,0:T(8,128)(2,1)S(1)}, bf16[64,384]{1,0:T(8,128)(2,1)S(1)}, u32[]{:S(2)}, u32[]{:S(2)}) %collective-permute-start) | collective-permute-done | bytes 49184 | tf_op jit(solution)/shard_map/ppermute | solution.py:326
  34.4 12.6 %all-to-all-done.recv_ref = bf16[128,16,128]{2,1,0:T(8,128)(2,1)S(1)} async-done(((bf16[128,16,128]{2,1,0:T(8,128)(2,1)}), bf16[128,16,128]{2,1,0:T(8,128)(2,1)S(1)}, u32[]{:S(2)}, u32[]{:S(2)}) %all-to-all-start) | async-done | bytes 524320 | tf_op jit(solution)/shard_map/all_to_all | solution.py:317
  47.0 2.8 %col_scan.1 = (bf16[4,96,128]{2,1,0:T(8,128)(2,1)S(1)}, f32[128,8,128]{2,1,0:T(8,128)S(1)}, f32[16,128]{1,0:T(8,128)S(1)}, f32[32,384]{1,0:T(8,128)S(1)}, bf16[32,384]{1,0:T(8,128)(2,1)S(1)}) custom-call(bf16[128,16,128]{2,1,0:T(8,128)(2,1)S(1)} %all-to-all-done.recv_ref, f32[64,384]{1,0:T(8,128)S(1)} %get-tuple-element.22.own_ref, ...), custom_call_target="tpu_custom_call" | custom-call | flops 1000000000 | bytes 1000000 | tf_op jit(solution)/shard_map/col_scan/pallas_call | solution.py:329
  49.8 6.6 %all_to_all.15.hop_ref = bf16[4,96,128]{2,1,0:T(8,128)(2,1)S(1)} all-to-all(bf16[4,96,128]{2,1,0:T(8,128)(2,1)S(1)} %get-tuple-element.24), channel_id=1, replica_groups=mesh['rows'=128,'heads'=4] {'heads'}, dimensions={0} | all-to-all | bytes 196608 | tf_op jit(solution)/shard_map/all_to_all | solution.py:335
  56.3 0.8 pack_cols.1
  57.2 7.4 %all-to-all-start.2 = ((bf16[128,8,128]{2,1,0:T(8,128)(2,1)}), bf16[128,8,128]{2,1,0:T(8,128)(2,1)S(1)}, u32[]{:S(2)}, u32[]{:S(2)}) async-start(bf16[128,8,128]{2,1,0:T(8,128)(2,1)} %pack_cols.1), calls=%async_computation.2 | async-start | bytes 524288 | tf_op jit(solution)/shard_map/all_to_all | solution.py:343
  64.6 2.2 %collective-permute-start.1 = (bf16[32,384]{1,0:T(8,128)(2,1)S(1)}, bf16[32,384]{1,0:T(8,128)(2,1)S(1)}, u32[]{:S(2)}, u32[]{:S(2)}) collective-permute-start(bf16[32,384]{1,0:T(8,128)(2,1)S(1)} %get-tuple-element.29), channel_id=1, source_target_pairs={{0,2},{1,3},{2,0},{3,1},{4,6},{5,7},{6,4},{7,5},{8,10},{9,11},{10,... | collective-permute-start | bytes 73736 | tf_op jit(solution)/shard_map/ppermute | solution.py:336
  66.8 3.6 %collective-permute-done.1.other_ref = bf16[32,384]{1,0:T(8,128)(2,1)S(1)} collective-permute-done((bf16[32,384]{1,0:T(8,128)(2,1)S(1)}, bf16[32,384]{1,0:T(8,128)(2,1)S(1)}, u32[]{:S(2)}, u32[]{:S(2)}) %collective-permute-start.1) | collective-permute-done | bytes 24608 | tf_op jit(solution)/shard_map/ppermute | solution.py:336
  70.4 13.1 %all-to-all-done.2.back_ref = bf16[128,8,128]{2,1,0:T(8,128)(2,1)S(1)} async-done(((bf16[128,8,128]{2,1,0:T(8,128)(2,1)}), bf16[128,8,128]{2,1,0:T(8,128)(2,1)S(1)}, u32[]{:S(2)}, u32[]{:S(2)}) %all-to-all-start.2) | async-done | bytes 262176 | tf_op jit(solution)/shard_map/all_to_all | solution.py:343
  83.5 1.0 %join.1 = (bf16[256,384]{1,0:T(8,128)(2,1)}, bf16[16,384]{1,0:T(8,128)(2,1)}, bf16[16,384]{1,0:T(8,128)(2,1)}, bf16[16,384]{1,0:T(8,128)(2,1)}, bf16[16,384]{1,0:T(8,128)(2,1)}, /*index=5*/bf16[4,384]{1,0:T(4,128)(2,1)}) custom-call(bf16[128,8,128]{2,1,0:T(8,128)(2,1)S(1)} %all-to-all-done.2.back_ref, f32[256,384]{1,0:T(8,128)S(1)} %get-tuple-element.27.dx_ref, ...), custom_call_target="tpu_custom_call" | custom-call | flops 10000000 | bytes 1000000 | tf_op jit(solution)/shard_map/join/pallas_call | solution.py:344
Async XLA Ops:
  3.2 19.4 %copy-start = (bf16[256,1,384]{2,0,1:T(8,128)(2,1)S(1)}, bf16[256,1,384]{2,0,1:T(8,128)(2,1)}, u32[]{:S(2)}) copy-start(bf16[256,1,384]{2,0,1:T(8,128)(2,1)} %param.9) | copy-start | bytes 589828
  3.3 19.4 %copy-start.1 = (bf16[256,1,384]{2,0,1:T(8,128)(2,1)S(1)}, bf16[256,1,384]{2,0,1:T(8,128)(2,1)}, u32[]{:S(2)}) copy-start(bf16[256,1,384]{2,0,1:T(8,128)(2,1)} %param.10) | copy-start | bytes 589828
  3.3 19.4 %copy-start.3 = (bf16[64,1,384]{2,0,1:T(8,128)(2,1)S(1)}, bf16[64,1,384]{2,0,1:T(8,128)(2,1)}, u32[]{:S(2)}) copy-start(bf16[64,1,384]{2,0,1:T(8,128)(2,1)} %param.11) | copy-start | bytes 147460
  3.3 19.4 %copy-start.4 = (bf16[64,1,384]{2,0,1:T(8,128)(2,1)S(1)}, bf16[64,1,384]{2,0,1:T(8,128)(2,1)}, u32[]{:S(2)}) copy-start(bf16[64,1,384]{2,0,1:T(8,128)(2,1)} %param.12) | copy-start | bytes 147460
  3.3 43.7 %all-to-all-start = ((bf16[128,16,128]{2,1,0:T(8,128)(2,1)}), bf16[128,16,128]{2,1,0:T(8,128)(2,1)S(1)}, u32[]{:S(2)}, u32[]{:S(2)}) async-start(bf16[128,16,128]{2,1,0:T(8,128)(2,1)} %pack_rows.1), calls=%async_computation | async-start | bytes 1048576 | tf_op jit(solution)/shard_map/all_to_all | solution.py:317
  22.6 0.7 copy-start.5
  22.6 0.7 copy-start.2
  26.6 7.8 %collective-permute-start = (bf16[64,384]{1,0:T(8,128)(2,1)S(1)}, bf16[64,384]{1,0:T(8,128)(2,1)S(1)}, u32[]{:S(2)}, u32[]{:S(2)}) collective-permute-start(bf16[64,384]{1,0:T(8,128)(2,1)S(1)} %get-tuple-element.23), channel_id=1, source_target_pairs={{0,1},{1,0},{2,3},{3,2},{4,5},{5,4},{6,7},{7,6},{8,9},{9,8},{10,11... | collective-permute-start | bytes 147464 | tf_op jit(solution)/shard_map/ppermute | solution.py:326
  57.2 26.3 %all-to-all-start.2 = ((bf16[128,8,128]{2,1,0:T(8,128)(2,1)}), bf16[128,8,128]{2,1,0:T(8,128)(2,1)S(1)}, u32[]{:S(2)}, u32[]{:S(2)}) async-start(bf16[128,8,128]{2,1,0:T(8,128)(2,1)} %pack_cols.1), calls=%async_computation.2 | async-start | bytes 524288 | tf_op jit(solution)/shard_map/all_to_all | solution.py:343
  64.6 5.8 %collective-permute-start.1 = (bf16[32,384]{1,0:T(8,128)(2,1)S(1)}, bf16[32,384]{1,0:T(8,128)(2,1)S(1)}, u32[]{:S(2)}, u32[]{:S(2)}) collective-permute-start(bf16[32,384]{1,0:T(8,128)(2,1)S(1)} %get-tuple-element.29), channel_id=1, source_target_pairs={{0,2},{1,3},{2,0},{3,1},{4,6},{5,7},{6,4},{7,5},{8,10},{9,11},{10,... | collective-permute-start | bytes 73736 | tf_op jit(solution)/shard_map/ppermute | solution.py:336

commit v4 on v3

--- a/solution.py
+++ b/solution.py
@@ -29,6 +29,13 @@
     i = lax.broadcasted_iota(jnp.int32, (L, L), 0)
     j = lax.broadcasted_iota(jnp.int32, (L, L), 1)
     return (i <= j).astype(dtype)
+
+
+def shuffle(rows, times):
+    m = rows * times
+    i = lax.broadcasted_iota(jnp.int32, (m, m), 0)
+    c = lax.broadcasted_iota(jnp.int32, (m, m), 1)
+    return ((c // times == i % rows) & (c % times == i // rows)).astype(BF16)
 
 
 def head_lanes():
@@ -52,7 +59,7 @@
     return nn(rows, spread)[0:1]
 
 
-def prep_kernel(x_any, w_any, u_any, v_any, a_any, tis_any, send_any, x_ref, w_ref, u_ref, v_ref, a_ref, tis_ref, send_ref, scr, sems, out_sems):
+def prep_kernel(x_any, w_any, u_any, v_any, a_any, tis_any, send_any, x_ref, w_ref, u_ref, v_ref, a_ref, tis_ref, send_ref, sems, out_sems):
     n = x_ref.shape[1]
     blocks = n // L
     halves = x_ref.shape[0] // L
@@ -67,21 +74,22 @@
     for copy in copies[:4]:
         copy.wait()
     keep = keep_of(tis_ref[...], n).astype(BF16)
+    rows_of = [None] * (per * blocks + 1)
     for k in range(blocks):
         at = pl.ds(k * L, L)
         uv = jnp.concatenate([u_ref[:, at].astype(F32), v_ref[:, at].astype(F32)], axis=0)
-        scr[:, per * k + 2 * halves, :] = uv.T
+        rows_of[per * k + 2 * halves] = uv.T
     a = [a_ref[:, pl.ds(k * L, L)].astype(F32) for k in range(blocks)]
     a.append(jnp.zeros((L - heads * blocks, L), F32))
-    scr[:, per * blocks, :] = jnp.concatenate(a, axis=0).T
+    rows_of[per * blocks] = jnp.concatenate(a, axis=0).T
     for o, ref in ((0, x_ref), (halves, w_ref)):
         for r in range(halves):
             copies[4 + o + r].wait()
             for k in range(blocks):
                 at = pl.ds(k * L, L)
                 part = ref[pl.ds(r * L, L), at] * keep[:, k * L : (k + 1) * L]
-                scr[:, per * k + o + r, :] = part.T.astype(F32)
-    send_out(scr, send_ref, send_any, out_sems)
+                rows_of[per * k + o + r] = part.T.astype(F32)
+    send_tiles(rows_of, send_ref, send_any, out_sems)
 
 
 def send_out(src, mid, dst, sems):
@@ -95,6 +103,31 @@
         copies[-1].start()
     for copy in copies:
         copy.wait()
+
+
+def send_tiles(planes, mid, dst, sems):
+    rows, pieces = len(planes), sems.shape[0]
+    size = L // rows
+    order = shuffle(rows, size)
+    copies = []
+    for i in range(pieces):
+        for g in range(rows // pieces):
+            at = (i * (rows // pieces) + g) * size
+            mixed = jnp.concatenate([p[at : at + size] for p in planes], axis=0)
+            mid[pl.ds(at, size)] = nn(order, mixed.astype(BF16)).astype(BF16).reshape(size, rows, L)
+        at = pl.ds(i * (L // pieces), L // pieces)
+        copies.append(pltpu.make_async_copy(mid.at[at], dst.at[at], sems.at[i]))
+        copies[-1].start()
+    for copy in copies:
+        copy.wait()
+
+
+def planes_of(ref):
+    rows = ref.shape[1]
+    size = L // rows
+    order = shuffle(size, rows)
+    parts = [nn(order, ref[pl.ds(g * size, size)].reshape(L, L)) for g in range(rows)]
+    return [jnp.concatenate([p[j * size : (j + 1) * size] for p in parts], axis=0) for j in range(rows)]
 
 
 def row_kernel(x_ref, w_ref, tis_ref, u_ref, v_ref, a_ref, dx_ref, own_ref, give_ref, da_ref, y_ref, duv_ref, xm_ref, wm_ref, wt_ref):
@@ -178,18 +211,18 @@
         da_ref[:, at] = da.astype(BF16)
 
 
-def col_kernel(recv_ref, own_ref, near_ref, hop_ref, ret_ref, da_ref, mine_ref, pass_ref, scr, y_ref, dx_ref, *, blocks, heads):
+def col_kernel(recv_ref, own_ref, near_ref, hop_ref, ret_ref, da_ref, mine_ref, pass_ref, y_ref, dx_ref, *, blocks, heads):
     part = mine_ref.shape[0]
     mine_ref[...] = own_ref[:part] + near_ref[:part].astype(F32)
     pass_ref[...] = (own_ref[part:] + near_ref[part:].astype(F32)).astype(pass_ref.dtype)
-    scr[...] = recv_ref[...].astype(F32)
+    mat = planes_of(recv_ref)
     halves = heads // 2
     per = 2 * halves + 1
     half = head_lanes()
     i0 = lax.broadcasted_iota(jnp.int32, (L, L), 0)
     i1 = lax.broadcasted_iota(jnp.int32, (L, L), 1)
     later = i0 <= i1
-    gcol = nn((i1 <= i0).astype(BF16), scr[:, per * blocks, :].astype(BF16))
+    gcol = nn((i1 <= i0).astype(BF16), mat[per * blocks].astype(BF16))
     grow = gcol.T
     quarter = HD // 4
     rows = da_ref.shape[0]
@@ -198,13 +231,13 @@
     c1 = lax.broadcasted_iota(jnp.int32, (rows, width), 1)
     dg = jnp.zeros((rows, L), F32)
     for k in range(blocks):
-        uvt = scr[:, per * k + 2 * halves, :]
+        uvt = mat[per * k + 2 * halves]
         uv = uvt.T.astype(BF16)
         u, v = uv[:HD], uv[HD:]
         s = nn(uvt[:, :HD].astype(BF16), v)
         q = None
-        xs = [scr[:, per * k + r, :] for r in range(halves)]
-        ws = [scr[:, per * k + halves + r, :] for r in range(halves)]
+        xs = [mat[per * k + r] for r in range(halves)]
+        ws = [mat[per * k + halves + r] for r in range(halves)]
         for r in range(halves):
             pair = pl.ds(r * L, L)
             x, w = xs[r].astype(BF16), ws[r].astype(BF16)
@@ -309,7 +342,7 @@
         [(tile, BF16, "far")],
         [
             vm((chan, n), BF16), vm((chan, n), BF16), vm((nstate, n), BF16), vm((nstate, n), BF16),
-            vm((heads, n), BF16), vm(tissue.shape, jnp.int32), vm(tile, BF16), vm(tile, F32),
+            vm((heads, n), BF16), vm(tissue.shape, jnp.int32), vm(tile, BF16),
             dma((4 + 2 * chan // L,)), dma((4,)),
         ],
         10**7, "pack_rows", 60, [True] * 6,
@@ -329,7 +362,7 @@
     hop, ret, da_col, mine, give = call(
         partial(col_kernel, blocks=blocks, heads=heads),
         [((4, 2 * quarter * blocks, L), BF16), (back_tile, F32), ((16, L), F32), (share, F32), (share, BF16)],
-        [vm(tile, F32), vm((L, chan), F32), vm((L, chan), F32)],
+        [vm((L, chan), F32), vm((L, chan), F32)],
         10**9, "col_scan",
     )(recv, own, near)
     hopped = lax.all_to_all(hop, "heads", split_axis=0, concat_axis=0, tiled=True)

time: 84.9 us -> 84.1 us (level)
  Pallas kernels: 10.6 us -> 9.68 us
where the time goes in v4:
time: 84.1 us; the launch traced here: 83.7 us
  waiting for transfers between devices  34.2 us (41%)
  starting transfers between devices  31.8 us (38%)
  Pallas kernels  9.68 us (12%)
  blocking collectives  6.57 us (8%)
    all_to_all x1, starting transfers between devices, body(): recv = lax.all_to_all(send, 'rows', split_axis=0, concat_axis=0, tiled=True)  19.3 us
    all_to_all x1, waiting for transfers between devices, body(): lax.all_to_all(packed, 'rows', split_axis=0, concat_axis=0, tiled=True)  13.1 us
    all_to_all x1, waiting for transfers between devices, body(): recv = lax.all_to_all(send, 'rows', split_axis=0, concat_axis=0, tiled=True)  12.6 us
    all_to_all x1, starting transfers between devices, body(): lax.all_to_all(packed, 'rows', split_axis=0, concat_axis=0, tiled=True)  7.44 us
    all_to_all x1, blocking collectives, body(): lax.all_to_all(hop, 'heads', split_axis=0, concat_axis=0, tiled=True)  6.57 us
    ppermute x1, waiting for transfers between devices, body(): near = lax.ppermute(give, 'heads', [(i, i ^ 1) for i in range(4)])  4.87 us
    ppermute x1, waiting for transfers between devices, body(): other = lax.ppermute(give, 'heads', [(i, i ^ 2) for i in range(4)])  3.6 us
    pallas_call x1, Pallas kernels, body(): call(row_kernel, [((chan, n), F32), (two, F32), (two, BF16), ((heads, n),...  3.27 us
  transfers between devices with their start and end apart: 4, of which 4 were waited for; matrix products, arithmetic and copies ran while one was open for 0% of the time, Pallas kernels for 4%

profile of v4, /device:TPU:9, one launch (start us, length us, event | category | flops | bytes accessed | tf_op | source)
XLA Modules:
  0.0 83.7 jit_solution(13972792803724491719)
XLA Ops:
  0.6 2.4 %pack_rows.1 = bf16[128,16,128]{2,1,0:T(8,128)(2,1)} custom-call(bf16[256,384]{1,0:T(8,128)(2,1)} %bitcast.15, bf16[256,384]{1,0:T(8,128)(2,1)} %bitcast.17, bf16[64,384]{1,0:T(8,128)(2,1)} %bitcast.22, bf16[64,384]{1,0:T(8,128)(2,1)} %bitcast.23, bf16[4,384]{1,0:T(4,128)(2,1)} %bitcast.24, s32[1,24]{1,0:T(1,128)} %tis_ref.3), custom_call_target="tpu_custom_call" | custom-call | flops 10000000 | bytes 1000000 | tf_op jit(solution)/shard_map/pack_rows/pallas_call | solution.py:340
  3.1 0.0 copy-start
  3.1 0.0 copy-start.1
  3.1 0.0 copy-start.3
  3.1 0.0 copy-start.4
  3.1 19.3 %all-to-all-start = ((bf16[128,16,128]{2,1,0:T(8,128)(2,1)}), bf16[128,16,128]{2,1,0:T(8,128)(2,1)S(1)}, u32[]{:S(2)}, u32[]{:S(2)}) async-start(bf16[128,16,128]{2,1,0:T(8,128)(2,1)} %pack_rows.1), calls=%async_computation | async-start | bytes 1048576 | tf_op jit(solution)/shard_map/all_to_all | solution.py:350
  22.4 0.0 copy-start.5
  22.4 0.0 copy-start.2
  22.4 0.0 copy-done
  22.4 0.0 copy-done.1
  22.4 0.0 copy-done.3
  22.5 0.0 copy-done.4
  22.5 0.6 copy-done.5
  23.1 0.0 copy-done.2
  23.1 3.3 %row_scan.1 = (f32[256,384]{1,0:T(8,128)S(1)}, f32[64,384]{1,0:T(8,128)S(1)}, bf16[64,384]{1,0:T(8,128)(2,1)S(1)}, bf16[4,384]{1,0:T(4,128)(2,1)}) custom-call(bf16[256,384]{1,0:T(8,128)(2,1)S(1)} %bitcast.16, bf16[256,384]{1,0:T(8,128)(2,1)S(1)} %bitcast.18, s32[1,24]{1,0:T(1,128)S(1)} %copy-done.2, bf16[64,384]{1,0:T(8,128)(2,1)S(1)} %bitcast.19, ...), custom_call_target="tpu_custom_call" | custom-call | flops 4000000000 | bytes 1000000 | tf_op jit(solution)/shard_map/row_scan/pallas_call | solution.py:353
  26.4 3.0 %collective-permute-start = (bf16[64,384]{1,0:T(8,128)(2,1)S(1)}, bf16[64,384]{1,0:T(8,128)(2,1)S(1)}, u32[]{:S(2)}, u32[]{:S(2)}) collective-permute-start(bf16[64,384]{1,0:T(8,128)(2,1)S(1)} %get-tuple-element.23), channel_id=1, source_target_pairs={{0,1},{1,0},{2,3},{3,2},{4,5},{5,4},{6,7},{7,6},{8,9},{9,8},{10,11... | collective-permute-start | bytes 147464 | tf_op jit(solution)/shard_map/ppermute | solution.py:359
  29.3 4.9 %collective-permute-done.near_ref = bf16[64,384]{1,0:T(8,128)(2,1)S(1)} collective-permute-done((bf16[64,384]{1,0:T(8,128)(2,1)S(1)}, bf16[64,384]{1,0:T(8,128)(2,1)S(1)}, u32[]{:S(2)}, u32[]{:S(2)}) %collective-permute-start) | collective-permute-done | bytes 49184 | tf_op jit(solution)/shard_map/ppermute | solution.py:359
  34.2 12.6 %all-to-all-done.recv_ref = bf16[128,16,128]{2,1,0:T(8,128)(2,1)S(1)} async-done(((bf16[128,16,128]{2,1,0:T(8,128)(2,1)}), bf16[128,16,128]{2,1,0:T(8,128)(2,1)S(1)}, u32[]{:S(2)}, u32[]{:S(2)}) %all-to-all-start) | async-done | bytes 524320 | tf_op jit(solution)/shard_map/all_to_all | solution.py:350
  46.8 2.1 %col_scan.1 = (bf16[4,96,128]{2,1,0:T(8,128)(2,1)S(1)}, f32[128,8,128]{2,1,0:T(8,128)S(1)}, f32[16,128]{1,0:T(8,128)S(1)}, f32[32,384]{1,0:T(8,128)S(1)}, bf16[32,384]{1,0:T(8,128)(2,1)S(1)}) custom-call(bf16[128,16,128]{2,1,0:T(8,128)(2,1)S(1)} %all-to-all-done.recv_ref, f32[64,384]{1,0:T(8,128)S(1)} %get-tuple-element.22.own_ref, ...), custom_call_target="tpu_custom_call" | custom-call | flops 1000000000 | bytes 1000000 | tf_op jit(solution)/shard_map/col_scan/pallas_call | solution.py:362
  48.9 6.6 %all_to_all.15.hop_ref = bf16[4,96,128]{2,1,0:T(8,128)(2,1)S(1)} all-to-all(bf16[4,96,128]{2,1,0:T(8,128)(2,1)S(1)} %get-tuple-element.24), channel_id=1, replica_groups=mesh['rows'=128,'heads'=4] {'heads'}, dimensions={0} | all-to-all | bytes 196608 | tf_op jit(solution)/shard_map/all_to_all | solution.py:368
  55.4 0.8 %pack_cols.1 = bf16[128,8,128]{2,1,0:T(8,128)(2,1)} custom-call(bf16[4,96,128]{2,1,0:T(8,128)(2,1)S(1)} %all_to_all.15.hop_ref, f32[128,8,128]{2,1,0:T(8,128)S(1)} %get-tuple-element.25.ret_ref, f32[16,128]{1,0:T(8,128)S(1)} %get-tuple-element.26.da_ref), custom_call_target="tpu_custom_call" | custom-call | flops 10000000 | bytes 1000000 | tf_op jit(solution)/shard_map/pack_cols/pallas_call | solution.py:370
  56.3 7.4 %all-to-all-start.2 = ((bf16[128,8,128]{2,1,0:T(8,128)(2,1)}), bf16[128,8,128]{2,1,0:T(8,128)(2,1)S(1)}, u32[]{:S(2)}, u32[]{:S(2)}) async-start(bf16[128,8,128]{2,1,0:T(8,128)(2,1)} %pack_cols.1), calls=%async_computation.2 | async-start | bytes 524288 | tf_op jit(solution)/shard_map/all_to_all | solution.py:376
  63.7 2.2 %collective-permute-start.1 = (bf16[32,384]{1,0:T(8,128)(2,1)S(1)}, bf16[32,384]{1,0:T(8,128)(2,1)S(1)}, u32[]{:S(2)}, u32[]{:S(2)}) collective-permute-start(bf16[32,384]{1,0:T(8,128)(2,1)S(1)} %get-tuple-element.29), channel_id=1, source_target_pairs={{0,2},{1,3},{2,0},{3,1},{4,6},{5,7},{6,4},{7,5},{8,10},{9,11},{10,... | collective-permute-start | bytes 73736 | tf_op jit(solution)/shard_map/ppermute | solution.py:369
  65.9 3.6 %collective-permute-done.1.other_ref = bf16[32,384]{1,0:T(8,128)(2,1)S(1)} collective-permute-done((bf16[32,384]{1,0:T(8,128)(2,1)S(1)}, bf16[32,384]{1,0:T(8,128)(2,1)S(1)}, u32[]{:S(2)}, u32[]{:S(2)}) %collective-permute-start.1) | collective-permute-done | bytes 24608 | tf_op jit(solution)/shard_map/ppermute | solution.py:369
  69.5 13.1 %all-to-all-done.2.back_ref = bf16[128,8,128]{2,1,0:T(8,128)(2,1)S(1)} async-done(((bf16[128,8,128]{2,1,0:T(8,128)(2,1)}), bf16[128,8,128]{2,1,0:T(8,128)(2,1)S(1)}, u32[]{:S(2)}, u32[]{:S(2)}) %all-to-all-start.2) | async-done | bytes 262176 | tf_op jit(solution)/shard_map/all_to_all | solution.py:376
  82.6 1.0 %join.1 = (bf16[256,384]{1,0:T(8,128)(2,1)}, bf16[16,384]{1,0:T(8,128)(2,1)}, bf16[16,384]{1,0:T(8,128)(2,1)}, bf16[16,384]{1,0:T(8,128)(2,1)}, bf16[16,384]{1,0:T(8,128)(2,1)}, /*index=5*/bf16[4,384]{1,0:T(4,128)(2,1)}) custom-call(bf16[128,8,128]{2,1,0:T(8,128)(2,1)S(1)} %all-to-all-done.2.back_ref, f32[256,384]{1,0:T(8,128)S(1)} %get-tuple-element.27.dx_ref, ...), custom_call_target="tpu_custom_call" | custom-call | flops 10000000 | bytes 1000000 | tf_op jit(solution)/shard_map/join/pallas_call | solution.py:377
Async XLA Ops:
  3.1 19.4 %copy-start = (bf16[256,1,384]{2,0,1:T(8,128)(2,1)S(1)}, bf16[256,1,384]{2,0,1:T(8,128)(2,1)}, u32[]{:S(2)}) copy-start(bf16[256,1,384]{2,0,1:T(8,128)(2,1)} %param.9) | copy-start | bytes 589828
  3.1 19.4 %copy-start.1 = (bf16[256,1,384]{2,0,1:T(8,128)(2,1)S(1)}, bf16[256,1,384]{2,0,1:T(8,128)(2,1)}, u32[]{:S(2)}) copy-start(bf16[256,1,384]{2,0,1:T(8,128)(2,1)} %param.10) | copy-start | bytes 589828
  3.1 19.4 %copy-start.3 = (bf16[64,1,384]{2,0,1:T(8,128)(2,1)S(1)}, bf16[64,1,384]{2,0,1:T(8,128)(2,1)}, u32[]{:S(2)}) copy-start(bf16[64,1,384]{2,0,1:T(8,128)(2,1)} %param.11) | copy-start | bytes 147460
  3.1 19.4 %copy-start.4 = (bf16[64,1,384]{2,0,1:T(8,128)(2,1)S(1)}, bf16[64,1,384]{2,0,1:T(8,128)(2,1)}, u32[]{:S(2)}) copy-start(bf16[64,1,384]{2,0,1:T(8,128)(2,1)} %param.12) | copy-start | bytes 147460
  3.1 43.7 %all-to-all-start = ((bf16[128,16,128]{2,1,0:T(8,128)(2,1)}), bf16[128,16,128]{2,1,0:T(8,128)(2,1)S(1)}, u32[]{:S(2)}, u32[]{:S(2)}) async-start(bf16[128,16,128]{2,1,0:T(8,128)(2,1)} %pack_rows.1), calls=%async_computation | async-start | bytes 1048576 | tf_op jit(solution)/shard_map/all_to_all | solution.py:350
  22.4 0.7 copy-start.5
  22.4 0.7 copy-start.2
  26.4 7.8 %collective-permute-start = (bf16[64,384]{1,0:T(8,128)(2,1)S(1)}, bf16[64,384]{1,0:T(8,128)(2,1)S(1)}, u32[]{:S(2)}, u32[]{:S(2)}) collective-permute-start(bf16[64,384]{1,0:T(8,128)(2,1)S(1)} %get-tuple-element.23), channel_id=1, source_target_pairs={{0,1},{1,0},{2,3},{3,2},{4,5},{5,4},{6,7},{7,6},{8,9},{9,8},{10,11... | collective-permute-start | bytes 147464 | tf_op jit(solution)/shard_map/ppermute | solution.py:359
  56.3 26.3 %all-to-all-start.2 = ((bf16[128,8,128]{2,1,0:T(8,128)(2,1)}), bf16[128,8,128]{2,1,0:T(8,128)(2,1)S(1)}, u32[]{:S(2)}, u32[]{:S(2)}) async-start(bf16[128,8,128]{2,1,0:T(8,128)(2,1)} %pack_cols.1), calls=%async_computation.2 | async-start | bytes 524288 | tf_op jit(solution)/shard_map/all_to_all | solution.py:376
  63.7 5.8 %collective-permute-start.1 = (bf16[32,384]{1,0:T(8,128)(2,1)S(1)}, bf16[32,384]{1,0:T(8,128)(2,1)S(1)}, u32[]{:S(2)}, u32[]{:S(2)}) collective-permute-start(bf16[32,384]{1,0:T(8,128)(2,1)S(1)} %get-tuple-element.29), channel_id=1, source_target_pairs={{0,2},{1,3},{2,0},{3,1},{4,6},{5,7},{6,4},{7,5},{8,10},{9,11},{10,... | collective-permute-start | bytes 73736 | tf_op jit(solution)/shard_map/ppermute | solution.py:369

commit v5 on v4

--- a/solution.py
+++ b/solution.py
@@ -130,7 +130,7 @@
     return [jnp.concatenate([p[j * size : (j + 1) * size] for p in parts], axis=0) for j in range(rows)]
 
 
-def row_kernel(x_ref, w_ref, tis_ref, u_ref, v_ref, a_ref, dx_ref, own_ref, give_ref, da_ref, y_ref, duv_ref, xm_ref, wm_ref, wt_ref):
+def row_kernel(x_ref, w_ref, tis_ref, u_ref, v_ref, a_ref, dx_ref, d0_ref, d1_ref, d2_ref, d3_ref, da_ref, y_ref, duv_ref, xm_ref, wm_ref, wt_ref):
     n = x_ref.shape[1]
     keep = keep_of(tis_ref[...], n).astype(BF16)
     xm_ref[...] = x_ref[...] * keep
@@ -193,12 +193,9 @@
             duv_ref[pl.ds(2 * quarter * k, quarter), at] = du[b][quarter * k : quarter * (k + 1)]
             duv_ref[pl.ds(2 * quarter * k + quarter, quarter), at] = dv[b][quarter * k : quarter * (k + 1)]
     me = lax.axis_index("heads")
-    part = 2 * quarter
-    for slot, near in enumerate((me, lax.rem(me + 2, 4))):
-        far = near + 1 - 2 * lax.rem(near, 2)
-        to = pl.ds(slot * part, part)
-        own_ref[to, :] = duv_ref[pl.ds(pl.multiple_of(near * part, part), part), :]
-        give_ref[to, :] = duv_ref[pl.ds(pl.multiple_of(far * part, part), part), :].astype(give_ref.dtype)
+    for shift, ref in enumerate((d0_ref, d1_ref, d2_ref, d3_ref)):
+        part = lax.rem(me + shift, 4) * (2 * quarter)
+        ref[...] = duv_ref[pl.ds(pl.multiple_of(part, 2 * quarter), 2 * quarter), :].astype(ref.dtype)
     suffix = (i0 >= i1).astype(BF16)
     later = jnp.zeros((heads, 1), F32)
     for b in reversed(range(blocks)):
@@ -211,10 +208,7 @@
         da_ref[:, at] = da.astype(BF16)
 
 
-def col_kernel(recv_ref, own_ref, near_ref, hop_ref, ret_ref, da_ref, mine_ref, pass_ref, y_ref, dx_ref, *, blocks, heads):
-    part = mine_ref.shape[0]
-    mine_ref[...] = own_ref[:part] + near_ref[:part].astype(F32)
-    pass_ref[...] = (own_ref[part:] + near_ref[part:].astype(F32)).astype(pass_ref.dtype)
+def col_kernel(recv_ref, after_ref, hop_ref, ret_ref, da_ref, y_ref, dx_ref, *, blocks, heads):
     mat = planes_of(recv_ref)
     halves = heads // 2
     per = 2 * halves + 1
@@ -284,7 +278,7 @@
     send_out(scr, out_ref, out_any, sems)
 
 
-def final_kernel(back_ref, dx_ref, tis_ref, mine_ref, other_ref, gx_ref, iu_ref, iv_ref, cu_ref, cv_ref, da_ref, scr, *, heads):
+def final_kernel(back_ref, dx_ref, tis_ref, r0_ref, r1_ref, r2_ref, r3_ref, gx_ref, iu_ref, iv_ref, cu_ref, cv_ref, da_ref, scr, *, heads):
     n = dx_ref.shape[1]
     blocks = n // L
     halves = heads // 2
@@ -305,7 +299,7 @@
         cv_ref[:, at] = small[o + quarter : o + 2 * quarter].astype(BF16)
         o = 2 * quarter * blocks + heads * k
         da_ref[:, at] = small[o : o + heads].astype(BF16)
-    row = mine_ref[...] + other_ref[...].astype(F32)
+    row = r0_ref[...] + r1_ref[...].astype(F32) + r2_ref[...].astype(F32) + r3_ref[...].astype(F32)
     iu_ref[...] = row[:quarter].astype(BF16)
     iv_ref[...] = row[quarter:].astype(BF16)
 
@@ -349,24 +343,24 @@
     )(x, w, flat(inject_col), flat(readout_col), flat(decay_col), tissue)
     recv = lax.all_to_all(send, "rows", split_axis=0, concat_axis=0, tiled=True)
     share = (2 * quarter, n)
-    two = (4 * quarter, n)
-    dx_row, own, give, da_row = call(
+    dx_row, mine, *theirs, da_row = call(
         row_kernel,
-        [((chan, n), F32), (two, F32), (two, BF16), ((heads, n), BF16)],
+        [((chan, n), F32), (share, F32), (share, BF16), (share, BF16), (share, BF16), ((heads, n), BF16)],
         [vm((chan, n), F32), vm((2 * nstate, n), F32), vm((chan, n), BF16), vm((chan, n), BF16), vm((n, chan), BF16)],
         4 * 10**9, "row_scan",
     )(x, w, tissue, flat(inject_row), flat(readout_row), flat(decay_row))
-    near = lax.ppermute(give, "heads", [(i, i ^ 1) for i in range(4)])
+    shares = [
+        lax.ppermute(part, "heads", [(i, (i + shift) % 4) for i in range(4)]) for shift, part in enumerate(theirs, 1)
+    ]
     used = blocks * heads // 2
     back_tile = (L, used + 2, L)
-    hop, ret, da_col, mine, give = call(
+    hop, ret, da_col = call(
         partial(col_kernel, blocks=blocks, heads=heads),
-        [((4, 2 * quarter * blocks, L), BF16), (back_tile, F32), ((16, L), F32), (share, F32), (share, BF16)],
+        [((4, 2 * quarter * blocks, L), BF16), (back_tile, F32), ((16, L), F32)],
         [vm((L, chan), F32), vm((L, chan), F32)],
         10**9, "col_scan",
-    )(recv, own, near)
+    )(recv, da_row)
     hopped = lax.all_to_all(hop, "heads", split_axis=0, concat_axis=0, tiled=True)
-    other = lax.ppermute(give, "heads", [(i, i ^ 2) for i in range(4)])
     (packed,) = call(
         partial(pack_kernel, used=used),
         [(back_tile, BF16, "far")],
@@ -379,7 +373,7 @@
         [((chan, n), BF16)] + [((quarter, n), BF16)] * 4 + [((heads, n), BF16)],
         [vm(back_tile, F32)],
         10**7, "join",
-    )(back, dx_row, tissue, mine, other)
+    )(back, dx_row, tissue, mine, *shares)
     wide = lambda x: x.reshape(x.shape[0], 1, n)
     return wide(gx), wide(iu), wide(iv), wide(cu), wide(cv), wide(da_row), wide(da)
 

time: 84.1 us -> 84.3 us (level)
  waiting for transfers between devices: 34.2 us -> 30.8 us
  starting transfers between devices: 31.8 us -> 34.7 us
    all_to_all x1, waiting for transfers between devices: 12.6 us -> 20.4 us  [body(): recv = lax.all_to_all(send, 'rows', split_axis=0, concat_axis=0, tiled=True)]
    all_to_all x1, waiting for transfers between devices: 13.1 us -> 6.66 us  [body(): lax.all_to_all(packed, 'rows', split_axis=0, concat_axis=0, tiled=True)]
    ppermute x2 -> x3, waiting for transfers between devices: 8.47 us -> 3.74 us  [body(): lax.ppermute(part, 'heads', [(i, (i + shift) % 4) for i in range(4)])]
    ppermute x2 -> x3, starting transfers between devices: 5.12 us -> 8.5 us  [body(): lax.ppermute(part, 'heads', [(i, (i + shift) % 4) for i in range(4)])]
  transfers between devices with their start and end apart: 4 -> 5, of which waited for: 4 -> 3; matrix products, arithmetic and copies ran while one was open for 0% -> 0% of each run, Pallas kernels for 4% -> 4%
where the time goes in v5:
time: 84.3 us; the launch traced here: 83.9 us
  starting transfers between devices  34.7 us (41%)
  waiting for transfers between devices  30.8 us (37%)
  Pallas kernels  9.66 us (11%)
  blocking collectives  6.64 us (8%)
  local copies, waits for them, and re-layouts  1.34 us (2%)
    all_to_all x1, waiting for transfers between devices, body(): recv = lax.all_to_all(send, 'rows', split_axis=0, concat_axis=0, tiled=True)  20.4 us
    all_to_all x1, starting transfers between devices, body(): recv = lax.all_to_all(send, 'rows', split_axis=0, concat_axis=0, tiled=True)  19.3 us
    ppermute x3, starting transfers between devices, body(): lax.ppermute(part, 'heads', [(i, (i + shift) % 4) for i in range(4)])  8.5 us
    all_to_all x1, starting transfers between devices, body(): lax.all_to_all(packed, 'rows', split_axis=0, concat_axis=0, tiled=True)  6.88 us
    all_to_all x1, waiting for transfers between devices, body(): lax.all_to_all(packed, 'rows', split_axis=0, concat_axis=0, tiled=True)  6.66 us
    all_to_all x1, blocking collectives, body(): lax.all_to_all(hop, 'heads', split_axis=0, concat_axis=0, tiled=True)  6.64 us
    ppermute x3, waiting for transfers between devices, body(): lax.ppermute(part, 'heads', [(i, (i + shift) % 4) for i in range(4)])  3.74 us
    pallas_call x1, Pallas kernels, body(): call(row_kernel, [((chan, n), F32), (share, F32), (share, BF16), (share,...  3.27 us
  transfers between devices with their start and end apart: 5, of which 3 were waited for; matrix products, arithmetic and copies ran while one was open for 0% of the time, Pallas kernels for 4%

profile of v5, /device:TPU:9, one launch (start us, length us, event | category | flops | bytes accessed | tf_op | source)
XLA Modules:
  0.0 83.9 jit_solution(687982176509972503)
XLA Ops:
  0.6 2.4 %pack_rows.1 = bf16[128,16,128]{2,1,0:T(8,128)(2,1)} custom-call(bf16[256,384]{1,0:T(8,128)(2,1)} %bitcast.15, bf16[256,384]{1,0:T(8,128)(2,1)} %bitcast.17, bf16[64,384]{1,0:T(8,128)(2,1)} %bitcast.23, bf16[64,384]{1,0:T(8,128)(2,1)} %bitcast.24, bf16[4,384]{1,0:T(4,128)(2,1)} %bitcast.25, s32[1,24]{1,0:T(1,128)} %tis_ref.3), custom_call_target="tpu_custom_call" | custom-call | flops 10000000 | bytes 1000000 | tf_op jit(solution)/shard_map/pack_rows/pallas_call | solution.py:334
  3.1 0.0 copy-start
  3.1 0.0 copy-start.1
  3.1 0.0 copy-start.3
  3.1 0.0 copy-start.4
  3.1 19.3 %all-to-all-start = ((bf16[128,16,128]{2,1,0:T(8,128)(2,1)}), bf16[128,16,128]{2,1,0:T(8,128)(2,1)S(1)}, u32[]{:S(2)}, u32[]{:S(2)}) async-start(bf16[128,16,128]{2,1,0:T(8,128)(2,1)} %pack_rows.1), calls=%async_computation | async-start | bytes 1048576 | tf_op jit(solution)/shard_map/all_to_all | solution.py:344
  22.4 0.0 copy-start.5
  22.4 0.0 copy-start.2
  22.4 0.0 copy-done
  22.4 0.0 copy-done.1
  22.4 0.0 copy-done.3
  22.5 0.0 copy-done.4
  22.5 0.6 copy-done.5
  23.1 0.0 copy-done.2
  23.1 3.3 %row_scan.1 = (f32[256,384]{1,0:T(8,128)S(1)}, f32[32,384]{1,0:T(8,128)S(1)}, bf16[32,384]{1,0:T(8,128)(2,1)S(1)}, bf16[32,384]{1,0:T(8,128)(2,1)S(1)}, bf16[32,...) custom-call(bf16[256,384]{1,0:T(8,128)(2,1)S(1)} %bitcast.16, bf16[256,384]{1,0:T(8,128)(2,1)S(1)} %bitcast.18, ...), custom_call_target="tpu_custom_call" | custom-call | flops 4000000000 | bytes 1000000 | tf_op jit(solution)/shard_map/row_scan/pallas_call | solution.py:346
  26.4 20.4 %all-to-all-done.recv_ref = bf16[128,16,128]{2,1,0:T(8,128)(2,1)S(1)} async-done(((bf16[128,16,128]{2,1,0:T(8,128)(2,1)}), bf16[128,16,128]{2,1,0:T(8,128)(2,1)S(1)}, u32[]{:S(2)}, u32[]{:S(2)}) %all-to-all-start) | async-done | bytes 524320 | tf_op jit(solution)/shard_map/all_to_all | solution.py:344
  46.8 0.0 copy-start.6
  46.8 0.7 copy-done.6
  47.5 2.1 %col_scan.1 = (bf16[4,96,128]{2,1,0:T(8,128)(2,1)S(1)}, f32[128,8,128]{2,1,0:T(8,128)S(1)}, f32[16,128]{1,0:T(8,128)S(1)}) custom-call(bf16[128,16,128]{2,1,0:T(8,128)(2,1)S(1)} %all-to-all-done.recv_ref, bf16[4,384]{1,0:T(4,128)(2,1)S(1)} %copy-done.6), custom_call_target="tpu_custom_call" | custom-call | flops 1000000000 | bytes 1000000 | tf_op jit(solution)/shard_map/col_scan/pallas_call | solution.py:357
  49.6 6.6 %all_to_all.15.hop_ref = bf16[4,96,128]{2,1,0:T(8,128)(2,1)S(1)} all-to-all(bf16[4,96,128]{2,1,0:T(8,128)(2,1)S(1)} %get-tuple-element.23), channel_id=1, replica_groups=mesh['rows'=128,'heads'=4] {'heads'}, dimensions={0} | all-to-all | bytes 196608 | tf_op jit(solution)/shard_map/all_to_all | solution.py:363
  56.2 0.8 pack_cols.1
  57.0 6.9 %all-to-all-start.2 = ((bf16[128,8,128]{2,1,0:T(8,128)(2,1)}), bf16[128,8,128]{2,1,0:T(8,128)(2,1)S(1)}, u32[]{:S(2)}, u32[]{:S(2)}) async-start(bf16[128,8,128]{2,1,0:T(8,128)(2,1)} %pack_cols.1), calls=%async_computation.2 | async-start | bytes 524288 | tf_op jit(solution)/shard_map/all_to_all | solution.py:370
  63.9 1.9 %collective-permute-start = (bf16[32,384]{1,0:T(8,128)(2,1)S(1)}, bf16[32,384]{1,0:T(8,128)(2,1)S(1)}, u32[]{:S(2)}, u32[]{:S(2)}) collective-permute-start(bf16[32,384]{1,0:T(8,128)(2,1)S(1)} %get-tuple-element.28), channel_id=1, source_target_pairs={{0,1},{1,2},{2,3},{3,0},{4,5},{5,6},{6,7},{7,4},{8,9},{9,10},{10,1... | collective-permute-start | bytes 73736 | tf_op jit(solution)/shard_map/ppermute | solution.py:353
  65.9 4.7 %collective-permute-start.1 = (bf16[32,384]{1,0:T(8,128)(2,1)S(1)}, bf16[32,384]{1,0:T(8,128)(2,1)S(1)}, u32[]{:S(2)}, u32[]{:S(2)}) collective-permute-start(bf16[32,384]{1,0:T(8,128)(2,1)S(1)} %get-tuple-element.29), channel_id=1, source_target_pairs={{0,2},{1,3},{2,0},{3,1},{4,6},{5,7},{6,4},{7,5},{8,10},{9,11},{10,... | collective-permute-start | bytes 73736 | tf_op jit(solution)/shard_map/ppermute | solution.py:353
  70.5 1.9 %collective-permute-start.2 = (bf16[32,384]{1,0:T(8,128)(2,1)S(1)}, bf16[32,384]{1,0:T(8,128)(2,1)S(1)}, u32[]{:S(2)}, u32[]{:S(2)}) collective-permute-start(bf16[32,384]{1,0:T(8,128)(2,1)S(1)} %get-tuple-element.30), channel_id=1, source_target_pairs={{0,3},{1,0},{2,1},{3,2},{4,7},{5,4},{6,5},{7,6},{8,11},{9,8},{10,9... | collective-permute-start | bytes 73736 | tf_op jit(solution)/shard_map/ppermute | solution.py:353
  72.4 0.0 collective-permute-done.r1_ref
  72.5 0.0 collective-permute-done.1.r2_ref
  72.5 3.7 %collective-permute-done.2.r3_ref = bf16[32,384]{1,0:T(8,128)(2,1)S(1)} collective-permute-done((bf16[32,384]{1,0:T(8,128)(2,1)S(1)}, bf16[32,384]{1,0:T(8,128)(2,1)S(1)}, u32[]{:S(2)}, u32[]{:S(2)}) %collective-permute-start.2) | collective-permute-done | bytes 24608 | tf_op jit(solution)/shard_map/ppermute | solution.py:353
  76.2 6.7 %all-to-all-done.2.back_ref = bf16[128,8,128]{2,1,0:T(8,128)(2,1)S(1)} async-done(((bf16[128,8,128]{2,1,0:T(8,128)(2,1)}), bf16[128,8,128]{2,1,0:T(8,128)(2,1)S(1)}, u32[]{:S(2)}, u32[]{:S(2)}) %all-to-all-start.2) | async-done | bytes 262176 | tf_op jit(solution)/shard_map/all_to_all | solution.py:370
  82.9 1.0 %join.1 = (bf16[256,384]{1,0:T(8,128)(2,1)}, bf16[16,384]{1,0:T(8,128)(2,1)}, bf16[16,384]{1,0:T(8,128)(2,1)}, bf16[16,384]{1,0:T(8,128)(2,1)}, bf16[16,384]{1,0:T(8,128)(2,1)}, /*index=5*/bf16[4,384]{1,0:T(4,128)(2,1)}) custom-call(bf16[128,8,128]{2,1,0:T(8,128)(2,1)S(1)} %all-to-all-done.2.back_ref, f32[256,384]{1,0:T(8,128)S(1)} %get-tuple-element.26.dx_ref, ...), custom_call_target="tpu_custom_call" | custom-call | flops 10000000 | bytes 1000000 | tf_op jit(solution)/shard_map/join/pallas_call | solution.py:371
Async XLA Ops:
  3.1 19.4 %copy-start = (bf16[256,1,384]{2,0,1:T(8,128)(2,1)S(1)}, bf16[256,1,384]{2,0,1:T(8,128)(2,1)}, u32[]{:S(2)}) copy-start(bf16[256,1,384]{2,0,1:T(8,128)(2,1)} %param.9) | copy-start | bytes 589828
  3.1 19.4 %copy-start.1 = (bf16[256,1,384]{2,0,1:T(8,128)(2,1)S(1)}, bf16[256,1,384]{2,0,1:T(8,128)(2,1)}, u32[]{:S(2)}) copy-start(bf16[256,1,384]{2,0,1:T(8,128)(2,1)} %param.10) | copy-start | bytes 589828
  3.1 19.4 %copy-start.3 = (bf16[64,1,384]{2,0,1:T(8,128)(2,1)S(1)}, bf16[64,1,384]{2,0,1:T(8,128)(2,1)}, u32[]{:S(2)}) copy-start(bf16[64,1,384]{2,0,1:T(8,128)(2,1)} %param.11) | copy-start | bytes 147460
  3.1 19.4 %copy-start.4 = (bf16[64,1,384]{2,0,1:T(8,128)(2,1)S(1)}, bf16[64,1,384]{2,0,1:T(8,128)(2,1)}, u32[]{:S(2)}) copy-start(bf16[64,1,384]{2,0,1:T(8,128)(2,1)} %param.12) | copy-start | bytes 147460
  3.1 43.7 %all-to-all-start = ((bf16[128,16,128]{2,1,0:T(8,128)(2,1)}), bf16[128,16,128]{2,1,0:T(8,128)(2,1)S(1)}, u32[]{:S(2)}, u32[]{:S(2)}) async-start(bf16[128,16,128]{2,1,0:T(8,128)(2,1)} %pack_rows.1), calls=%async_computation | async-start | bytes 1048576 | tf_op jit(solution)/shard_map/all_to_all | solution.py:344
  22.4 0.7 copy-start.5
  22.4 0.7 copy-start.2
  46.8 0.7 copy-start.6
  57.0 25.8 %all-to-all-start.2 = ((bf16[128,8,128]{2,1,0:T(8,128)(2,1)}), bf16[128,8,128]{2,1,0:T(8,128)(2,1)S(1)}, u32[]{:S(2)}, u32[]{:S(2)}) async-start(bf16[128,8,128]{2,1,0:T(8,128)(2,1)} %pack_cols.1), calls=%async_computation.2 | async-start | bytes 524288 | tf_op jit(solution)/shard_map/all_to_all | solution.py:370
  63.9 8.5 %collective-permute-start = (bf16[32,384]{1,0:T(8,128)(2,1)S(1)}, bf16[32,384]{1,0:T(8,128)(2,1)S(1)}, u32[]{:S(2)}, u32[]{:S(2)}) collective-permute-start(bf16[32,384]{1,0:T(8,128)(2,1)S(1)} %get-tuple-element.28), channel_id=1, source_target_pairs={{0,1},{1,2},{2,3},{3,0},{4,5},{5,6},{6,7},{7,4},{8,9},{9,10},{10,1... | collective-permute-start | bytes 73736 | tf_op jit(solution)/shard_map/ppermute | solution.py:353
  65.9 6.6 %collective-permute-start.1 = (bf16[32,384]{1,0:T(8,128)(2,1)S(1)}, bf16[32,384]{1,0:T(8,128)(2,1)S(1)}, u32[]{:S(2)}, u32[]{:S(2)}) collective-permute-start(bf16[32,384]{1,0:T(8,128)(2,1)S(1)} %get-tuple-element.29), channel_id=1, source_target_pairs={{0,2},{1,3},{2,0},{3,1},{4,6},{5,7},{6,4},{7,5},{8,10},{9,11},{10,... | collective-permute-start | bytes 73736 | tf_op jit(solution)/shard_map/ppermute | solution.py:353
  70.5 5.7 %collective-permute-start.2 = (bf16[32,384]{1,0:T(8,128)(2,1)S(1)}, bf16[32,384]{1,0:T(8,128)(2,1)S(1)}, u32[]{:S(2)}, u32[]{:S(2)}) collective-permute-start(bf16[32,384]{1,0:T(8,128)(2,1)S(1)} %get-tuple-element.30), channel_id=1, source_target_pairs={{0,3},{1,0},{2,1},{3,2},{4,7},{5,4},{6,5},{7,6},{8,11},{9,8},{10,9... | collective-permute-start | bytes 73736 | tf_op jit(solution)/shard_map/ppermute | solution.py:353

commit v6 on v5

--- a/solution.py
+++ b/solution.py
@@ -359,7 +359,7 @@
         [((4, 2 * quarter * blocks, L), BF16), (back_tile, F32), ((16, L), F32)],
         [vm((L, chan), F32), vm((L, chan), F32)],
         10**9, "col_scan",
-    )(recv, da_row)
+    )(recv, mine)
     hopped = lax.all_to_all(hop, "heads", split_axis=0, concat_axis=0, tiled=True)
     (packed,) = call(
         partial(pack_kernel, used=used),

time: 84.3 us -> 83.6 us (level)
  no operation moved by 1% of the time
where the time goes in v6:
time: 83.6 us; the launch traced here: 83.2 us
  starting transfers between devices  34.7 us (42%)
  waiting for transfers between devices  30.8 us (37%)
  Pallas kernels  9.66 us (12%)
  blocking collectives  6.64 us (8%)
    all_to_all x1, waiting for transfers between devices, body(): recv = lax.all_to_all(send, 'rows', split_axis=0, concat_axis=0, tiled=True)  20.4 us
    all_to_all x1, starting transfers between devices, body(): recv = lax.all_to_all(send, 'rows', split_axis=0, concat_axis=0, tiled=True)  19.3 us
    ppermute x3, starting transfers between devices, body(): lax.ppermute(part, 'heads', [(i, (i + shift) % 4) for i in range(4)])  8.5 us
    all_to_all x1, starting transfers between devices, body(): lax.all_to_all(packed, 'rows', split_axis=0, concat_axis=0, tiled=True)  6.88 us
    all_to_all x1, waiting for transfers between devices, body(): lax.all_to_all(packed, 'rows', split_axis=0, concat_axis=0, tiled=True)  6.66 us
    all_to_all x1, blocking collectives, body(): lax.all_to_all(hop, 'heads', split_axis=0, concat_axis=0, tiled=True)  6.64 us
    ppermute x3, waiting for transfers between devices, body(): lax.ppermute(part, 'heads', [(i, (i + shift) % 4) for i in range(4)])  3.74 us
    pallas_call x1, Pallas kernels, body(): call(row_kernel, [((chan, n), F32), (share, F32), (share, BF16), (share,...  3.27 us
  transfers between devices with their start and end apart: 5, of which 3 were waited for; matrix products, arithmetic and copies ran while one was open for 0% of the time, Pallas kernels for 4%

profile of v6, /device:TPU:9, one launch (start us, length us, event | category | flops | bytes accessed | tf_op | source)
XLA Modules:
  0.0 83.2 jit_solution(10194198535369635284)
XLA Ops:
  0.6 2.4 %pack_rows.1 = bf16[128,16,128]{2,1,0:T(8,128)(2,1)} custom-call(bf16[256,384]{1,0:T(8,128)(2,1)} %bitcast.15, bf16[256,384]{1,0:T(8,128)(2,1)} %bitcast.17, bf16[64,384]{1,0:T(8,128)(2,1)} %bitcast.22, bf16[64,384]{1,0:T(8,128)(2,1)} %bitcast.23, bf16[4,384]{1,0:T(4,128)(2,1)} %bitcast.24, s32[1,24]{1,0:T(1,128)} %tis_ref.3), custom_call_target="tpu_custom_call" | custom-call | flops 10000000 | bytes 1000000 | tf_op jit(solution)/shard_map/pack_rows/pallas_call | solution.py:334
  3.1 0.0 copy-start
  3.1 0.0 copy-start.1
  3.1 0.0 copy-start.3
  3.1 0.0 copy-start.4
  3.1 19.3 %all-to-all-start = ((bf16[128,16,128]{2,1,0:T(8,128)(2,1)}), bf16[128,16,128]{2,1,0:T(8,128)(2,1)S(1)}, u32[]{:S(2)}, u32[]{:S(2)}) async-start(bf16[128,16,128]{2,1,0:T(8,128)(2,1)} %pack_rows.1), calls=%async_computation | async-start | bytes 1048576 | tf_op jit(solution)/shard_map/all_to_all | solution.py:344
  22.4 0.0 copy-start.5
  22.4 0.0 copy-start.2
  22.4 0.0 copy-done
  22.4 0.0 copy-done.1
  22.4 0.0 copy-done.3
  22.4 0.0 copy-done.4
  22.5 0.6 copy-done.5
  23.1 0.0 copy-done.2
  23.1 3.3 %row_scan.1 = (f32[256,384]{1,0:T(8,128)S(1)}, f32[32,384]{1,0:T(8,128)S(1)}, bf16[32,384]{1,0:T(8,128)(2,1)S(1)}, bf16[32,384]{1,0:T(8,128)(2,1)S(1)}, bf16[32,...) custom-call(bf16[256,384]{1,0:T(8,128)(2,1)S(1)} %bitcast.16, bf16[256,384]{1,0:T(8,128)(2,1)S(1)} %bitcast.18, ...), custom_call_target="tpu_custom_call" | custom-call | flops 4000000000 | bytes 1000000 | tf_op jit(solution)/shard_map/row_scan/pallas_call | solution.py:346
  26.4 20.4 %all-to-all-done.recv_ref = bf16[128,16,128]{2,1,0:T(8,128)(2,1)S(1)} async-done(((bf16[128,16,128]{2,1,0:T(8,128)(2,1)}), bf16[128,16,128]{2,1,0:T(8,128)(2,1)S(1)}, u32[]{:S(2)}, u32[]{:S(2)}) %all-to-all-start) | async-done | bytes 524320 | tf_op jit(solution)/shard_map/all_to_all | solution.py:344
  46.8 2.1 %col_scan.1 = (bf16[4,96,128]{2,1,0:T(8,128)(2,1)S(1)}, f32[128,8,128]{2,1,0:T(8,128)S(1)}, f32[16,128]{1,0:T(8,128)S(1)}) custom-call(bf16[128,16,128]{2,1,0:T(8,128)(2,1)S(1)} %all-to-all-done.recv_ref, f32[32,384]{1,0:T(8,128)S(1)} %get-tuple-element.22.after_ref.r0_ref), custom_call_target="tpu_custom_call" | custom-call | flops 1000000000 | bytes 1000000 | tf_op jit(solution)/shard_map/col_scan/pallas_call | solution.py:357
  48.9 6.6 %all_to_all.15.hop_ref = bf16[4,96,128]{2,1,0:T(8,128)(2,1)S(1)} all-to-all(bf16[4,96,128]{2,1,0:T(8,128)(2,1)S(1)} %get-tuple-element.23), channel_id=1, replica_groups=mesh['rows'=128,'heads'=4] {'heads'}, dimensions={0} | all-to-all | bytes 196608 | tf_op jit(solution)/shard_map/all_to_all | solution.py:363
  55.5 0.8 %pack_cols.1 = bf16[128,8,128]{2,1,0:T(8,128)(2,1)} custom-call(bf16[4,96,128]{2,1,0:T(8,128)(2,1)S(1)} %all_to_all.15.hop_ref, f32[128,8,128]{2,1,0:T(8,128)S(1)} %get-tuple-element.24.ret_ref, f32[16,128]{1,0:T(8,128)S(1)} %get-tuple-element.25.da_ref), custom_call_target="tpu_custom_call" | custom-call | flops 10000000 | bytes 1000000 | tf_op jit(solution)/shard_map/pack_cols/pallas_call | solution.py:364
  56.3 6.9 %all-to-all-start.2 = ((bf16[128,8,128]{2,1,0:T(8,128)(2,1)}), bf16[128,8,128]{2,1,0:T(8,128)(2,1)S(1)}, u32[]{:S(2)}, u32[]{:S(2)}) async-start(bf16[128,8,128]{2,1,0:T(8,128)(2,1)} %pack_cols.1), calls=%async_computation.2 | async-start | bytes 524288 | tf_op jit(solution)/shard_map/all_to_all | solution.py:370
  63.2 1.9 %collective-permute-start = (bf16[32,384]{1,0:T(8,128)(2,1)S(1)}, bf16[32,384]{1,0:T(8,128)(2,1)S(1)}, u32[]{:S(2)}, u32[]{:S(2)}) collective-permute-start(bf16[32,384]{1,0:T(8,128)(2,1)S(1)} %get-tuple-element.27), channel_id=1, source_target_pairs={{0,1},{1,2},{2,3},{3,0},{4,5},{5,6},{6,7},{7,4},{8,9},{9,10},{10,1... | collective-permute-start | bytes 73736 | tf_op jit(solution)/shard_map/ppermute | solution.py:353
  65.2 4.7 %collective-permute-start.1 = (bf16[32,384]{1,0:T(8,128)(2,1)S(1)}, bf16[32,384]{1,0:T(8,128)(2,1)S(1)}, u32[]{:S(2)}, u32[]{:S(2)}) collective-permute-start(bf16[32,384]{1,0:T(8,128)(2,1)S(1)} %get-tuple-element.28), channel_id=1, source_target_pairs={{0,2},{1,3},{2,0},{3,1},{4,6},{5,7},{6,4},{7,5},{8,10},{9,11},{10,... | collective-permute-start | bytes 73736 | tf_op jit(solution)/shard_map/ppermute | solution.py:353
  69.8 1.9 %collective-permute-start.2 = (bf16[32,384]{1,0:T(8,128)(2,1)S(1)}, bf16[32,384]{1,0:T(8,128)(2,1)S(1)}, u32[]{:S(2)}, u32[]{:S(2)}) collective-permute-start(bf16[32,384]{1,0:T(8,128)(2,1)S(1)} %get-tuple-element.29), channel_id=1, source_target_pairs={{0,3},{1,0},{2,1},{3,2},{4,7},{5,4},{6,5},{7,6},{8,11},{9,8},{10,9... | collective-permute-start | bytes 73736 | tf_op jit(solution)/shard_map/ppermute | solution.py:353
  71.8 0.0 collective-permute-done.r1_ref
  71.8 0.0 collective-permute-done.1.r2_ref
  71.8 3.7 %collective-permute-done.2.r3_ref = bf16[32,384]{1,0:T(8,128)(2,1)S(1)} collective-permute-done((bf16[32,384]{1,0:T(8,128)(2,1)S(1)}, bf16[32,384]{1,0:T(8,128)(2,1)S(1)}, u32[]{:S(2)}, u32[]{:S(2)}) %collective-permute-start.2) | collective-permute-done | bytes 24608 | tf_op jit(solution)/shard_map/ppermute | solution.py:353
  75.5 6.7 %all-to-all-done.2.back_ref = bf16[128,8,128]{2,1,0:T(8,128)(2,1)S(1)} async-done(((bf16[128,8,128]{2,1,0:T(8,128)(2,1)}), bf16[128,8,128]{2,1,0:T(8,128)(2,1)S(1)}, u32[]{:S(2)}, u32[]{:S(2)}) %all-to-all-start.2) | async-done | bytes 262176 | tf_op jit(solution)/shard_map/all_to_all | solution.py:370
  82.2 1.0 %join.1 = (bf16[256,384]{1,0:T(8,128)(2,1)}, bf16[16,384]{1,0:T(8,128)(2,1)}, bf16[16,384]{1,0:T(8,128)(2,1)}, bf16[16,384]{1,0:T(8,128)(2,1)}, bf16[16,384]{1,0:T(8,128)(2,1)}, /*index=5*/bf16[4,384]{1,0:T(4,128)(2,1)}) custom-call(bf16[128,8,128]{2,1,0:T(8,128)(2,1)S(1)} %all-to-all-done.2.back_ref, f32[256,384]{1,0:T(8,128)S(1)} %get-tuple-element.26.dx_ref, ...), custom_call_target="tpu_custom_call" | custom-call | flops 10000000 | bytes 1000000 | tf_op jit(solution)/shard_map/join/pallas_call | solution.py:371
Async XLA Ops:
  3.1 19.4 %copy-start = (bf16[256,1,384]{2,0,1:T(8,128)(2,1)S(1)}, bf16[256,1,384]{2,0,1:T(8,128)(2,1)}, u32[]{:S(2)}) copy-start(bf16[256,1,384]{2,0,1:T(8,128)(2,1)} %param.9) | copy-start | bytes 589828
  3.1 19.4 %copy-start.1 = (bf16[256,1,384]{2,0,1:T(8,128)(2,1)S(1)}, bf16[256,1,384]{2,0,1:T(8,128)(2,1)}, u32[]{:S(2)}) copy-start(bf16[256,1,384]{2,0,1:T(8,128)(2,1)} %param.10) | copy-start | bytes 589828
  3.1 19.4 %copy-start.3 = (bf16[64,1,384]{2,0,1:T(8,128)(2,1)S(1)}, bf16[64,1,384]{2,0,1:T(8,128)(2,1)}, u32[]{:S(2)}) copy-start(bf16[64,1,384]{2,0,1:T(8,128)(2,1)} %param.11) | copy-start | bytes 147460
  3.1 19.4 %copy-start.4 = (bf16[64,1,384]{2,0,1:T(8,128)(2,1)S(1)}, bf16[64,1,384]{2,0,1:T(8,128)(2,1)}, u32[]{:S(2)}) copy-start(bf16[64,1,384]{2,0,1:T(8,128)(2,1)} %param.12) | copy-start | bytes 147460
  3.1 43.7 %all-to-all-start = ((bf16[128,16,128]{2,1,0:T(8,128)(2,1)}), bf16[128,16,128]{2,1,0:T(8,128)(2,1)S(1)}, u32[]{:S(2)}, u32[]{:S(2)}) async-start(bf16[128,16,128]{2,1,0:T(8,128)(2,1)} %pack_rows.1), calls=%async_computation | async-start | bytes 1048576 | tf_op jit(solution)/shard_map/all_to_all | solution.py:344
  22.4 0.7 copy-start.5
  22.4 0.7 copy-start.2
  56.3 25.8 %all-to-all-start.2 = ((bf16[128,8,128]{2,1,0:T(8,128)(2,1)}), bf16[128,8,128]{2,1,0:T(8,128)(2,1)S(1)}, u32[]{:S(2)}, u32[]{:S(2)}) async-start(bf16[128,8,128]{2,1,0:T(8,128)(2,1)} %pack_cols.1), calls=%async_computation.2 | async-start | bytes 524288 | tf_op jit(solution)/shard_map/all_to_all | solution.py:370
  63.2 8.5 %collective-permute-start = (bf16[32,384]{1,0:T(8,128)(2,1)S(1)}, bf16[32,384]{1,0:T(8,128)(2,1)S(1)}, u32[]{:S(2)}, u32[]{:S(2)}) collective-permute-start(bf16[32,384]{1,0:T(8,128)(2,1)S(1)} %get-tuple-element.27), channel_id=1, source_target_pairs={{0,1},{1,2},{2,3},{3,0},{4,5},{5,6},{6,7},{7,4},{8,9},{9,10},{10,1... | collective-permute-start | bytes 73736 | tf_op jit(solution)/shard_map/ppermute | solution.py:353
  65.2 6.6 %collective-permute-start.1 = (bf16[32,384]{1,0:T(8,128)(2,1)S(1)}, bf16[32,384]{1,0:T(8,128)(2,1)S(1)}, u32[]{:S(2)}, u32[]{:S(2)}) collective-permute-start(bf16[32,384]{1,0:T(8,128)(2,1)S(1)} %get-tuple-element.28), channel_id=1, source_target_pairs={{0,2},{1,3},{2,0},{3,1},{4,6},{5,7},{6,4},{7,5},{8,10},{9,11},{10,... | collective-permute-start | bytes 73736 | tf_op jit(solution)/shard_map/ppermute | solution.py:353
  69.8 5.7 %collective-permute-start.2 = (bf16[32,384]{1,0:T(8,128)(2,1)S(1)}, bf16[32,384]{1,0:T(8,128)(2,1)S(1)}, u32[]{:S(2)}, u32[]{:S(2)}) collective-permute-start(bf16[32,384]{1,0:T(8,128)(2,1)S(1)} %get-tuple-element.29), channel_id=1, source_target_pairs={{0,3},{1,0},{2,1},{3,2},{4,7},{5,4},{6,5},{7,6},{8,11},{9,8},{10,9... | collective-permute-start | bytes 73736 | tf_op jit(solution)/shard_map/ppermute | solution.py:353
